TPU v7x, 256 devices: a whole 4x4x8 slice. The times are simulated.
256 devices in a mesh: seq: 2 (over x_hi), head: 2 (over core), dp: 64 (over z, y, x_lo).
Axes of the slice: x: 4 (x_hi: 2, x_lo: 2; x = x_hi * 2 + x_lo), y: 4, z: 8, core: 2. Of those that a mesh axis runs over, the one named last changes fastest.
Arguments:
- tokens: bfloat16 [64, 1024, 1536], P('dp', 'seq', 'head'), may hold values from -40 to 40
- lengths: int32 [64, 8], P('dp'), may hold values from 1 to 512, 1024 in all within a row
- owner_slot: int32 [64, 8], P('dp'), may hold values from 0 to 7, each once within a row
- latent_index: int32 [64, 8, 128], P('dp'), may hold values from 0 to 1048575
- cotangent: bfloat16 [64, 1024, 1536], P('dp', 'seq'), may hold values from -24 to 24
- qkv_weight: bfloat16 [3, 1536, 1536], P(None, None, 'head'), may hold values from -0.15625 to 0.15625
- out_weight: bfloat16 [1536, 1536], P('head'), may hold values from -1.25 to 1.25
Outputs:
- mixed: bfloat16 [64, 1024, 1536], P('dp', 'seq', 'head')
- latents: bfloat16 [64, 1024, 1536], P('dp', 'seq', 'head')
- grad_out: float32 [1536, 1536], P('head')
Inputs may be any that keep to these rules, and one draw needn't show every extreme that they name: Each pack's lengths sum to 1024.
All inputs are finite; a program needn't handle non-finite values.
Results may differ from a plain program's by a relative error of at most 0.013.
Values may be sent and summed in bfloat16 or wider, within the bound.
No kernel may reach another device: no remote copies, remote signals or barrier semaphores. Data moves between devices by JAX's collectives and lax.ppermute only.
A program may use at most 128 MiB of HBM per device.

v0:
```python
import functools

import jax
import jax.numpy as jnp
from jax import lax
from jax.experimental import pallas as pl
from jax.experimental.pallas import tpu as pltpu
from jax.sharding import Mesh
from jax.sharding import PartitionSpec as P

HD = 64
LAT = 128
IMAGES = 8
HEADER = 4
GROUP = 256
BIG = 128.0
EPS_NORM = 1e-05
EPS_HEAD = 1e-06
BF = jnp.bfloat16
F32 = jnp.float32
VMEM_LIMIT = 20 * 1024 * 1024
BIG_VMEM = 60 * 1024 * 1024


def norm_rows(head, own_ref, oth_ref, normed_ref):
    rows, share = own_ref.shape
    step = 128
    one = jnp.ones((share, 128), BF)
    row_sum = lambda a, b: jnp.dot(a, one, preferred_element_type=F32) + jnp.dot(b, one, preferred_element_type=F32)
    wide = lambda value: jnp.concatenate([value] * (share // 128), axis=1)
    own_at = pl.ds(pl.multiple_of(head * share, share), share)
    oth_at = pl.ds(pl.multiple_of((1 - head) * share, share), share)
    def block(i, carry):
        at = pl.ds(pl.multiple_of(i * step, step), step)
        mean = wide(row_sum(own_ref[at, :], oth_ref[at, :]) * (0.5 / share))
        own = own_ref[at, :].astype(F32) - mean
        oth = oth_ref[at, :].astype(F32) - mean
        var = row_sum((own * own).astype(BF), (oth * oth).astype(BF)) * (0.5 / share)
        scale = wide(lax.rsqrt(var + EPS_NORM))
        normed_ref[at, own_at] = (own * scale).astype(BF)
        normed_ref[at, oth_at] = (oth * scale).astype(BF)
        return carry

    lax.fori_loop(0, rows // step, block, 0)


def head_norm(values, ones):
    mean = jnp.dot((values * values).astype(BF), ones, preferred_element_type=F32)
    return values * lax.rsqrt(mean + EPS_HEAD)


def ones_block():
    row = lax.broadcasted_iota(jnp.int32, (GROUP, GROUP), 0) >> 6
    col = lax.broadcasted_iota(jnp.int32, (GROUP, GROUP), 1) >> 6
    return jnp.where(row == col, 1.0 / HD, 0.0).astype(BF)


def features(place_ref, first, rows, inside, constant):
    pos = first + lax.broadcasted_iota(jnp.int32, (rows, 128), 0)
    lane = lax.broadcasted_iota(jnp.int32, (1, 128), 1) & (HD - 1)
    starts = jnp.zeros((1, 128), jnp.int32)
    ends = jnp.zeros((1, 128), jnp.int32)
    end = jnp.int32(0)
    for i in range(IMAGES):
        starts = jnp.where(lane == i, end, starts)
        end = end + place_ref[HEADER + i]
        ends = jnp.where(lane == i, end, ends)
    member = (pos >= starts) & (pos < ends)
    return jnp.where(lane == IMAGES, constant, jnp.where(member, inside, 0.0)).astype(BF)


def lower_half(rows):
    return lax.broadcasted_iota(jnp.int32, (rows, 128), 1) < HD


def attend_group(q, k, v, qfeat, kfeat, emit):
    for pair in range(2):
        lanes = slice(pair * 128, pair * 128 + 128)
        qp, kp, vp = (q(lanes).astype(F32) * 0.125).astype(BF), k(lanes), v(lanes)
        qlow, klow = lower_half(qp.shape[0]), lower_half(kp.shape[0])
        one = jnp.ones_like(vp)
        for odd in range(2):
            qa = jnp.where(qlow, qfeat, qp) if odd else jnp.where(qlow, qp, qfeat)
            ka = jnp.where(klow, kfeat, kp) if odd else jnp.where(klow, kp, kfeat)
            va = jnp.where(klow, one, vp) if odd else jnp.where(klow, vp, one)
            s = lax.dot_general(qa, ka, (((1,), (1,)), ((), ())), preferred_element_type=F32)
            w = jnp.exp(s).astype(BF)
            emit(2 * pair + odd, jnp.dot(w, va, preferred_element_type=F32))


def local_kernel(place_ref, own_ref, oth_ref, w_ref, q_ref, acc_ref, normed_ref, qf_ref, kf_ref, wbuf_ref, qbuf_ref, abuf_ref, k_ref, v_ref, sems):
    rows = own_ref.shape[0]
    groups = wbuf_ref.shape[0]

    def load(g):
        lanes = pl.ds(pl.multiple_of(g * GROUP, GROUP), GROUP)
        return pltpu.make_async_copy(w_ref.at[:, :, lanes], wbuf_ref.at[g], sems.at[g])

    def stores(g):
        return (
            pltpu.make_async_copy(qbuf_ref.at[g], q_ref.at[g], sems.at[groups + g]),
            pltpu.make_async_copy(abuf_ref.at[g], acc_ref.at[g], sems.at[2 * groups + g]),
        )

    for g in range(groups):
        load(g).start()
    norm_rows(place_ref[1], own_ref, oth_ref, normed_ref)
    first = place_ref[0] * rows
    qf_ref[...] = features(place_ref, first, rows, BIG, -BIG)
    kf_ref[...] = features(place_ref, first, rows, 1.0, 1.0)

    def group(g, carry):
        load(g).wait()
        normed = normed_ref[...]
        ones = ones_block()
        qbuf_ref[g] = head_norm(jnp.dot(normed, wbuf_ref[g, 0], preferred_element_type=F32), ones).astype(BF)
        k_ref[...] = head_norm(jnp.dot(normed, wbuf_ref[g, 1], preferred_element_type=F32), ones).astype(BF)
        v_ref[...] = jnp.dot(normed, wbuf_ref[g, 2], preferred_element_type=F32).astype(BF)

        def emit(head, r):
            abuf_ref[g, :, head * 128 : head * 128 + 128] = r.astype(BF)

        attend_group(
            lambda lanes: qbuf_ref[g, :, lanes], lambda lanes: k_ref[:, lanes], lambda lanes: v_ref[:, lanes],
            qf_ref[...], kf_ref[...], emit,
        )
        for store in stores(g):
            store.start()
        return carry

    lax.fori_loop(0, groups, group, 0)
    for g in range(groups):
        for store in stores(g):
            store.wait()


def foreign_kernel(place_ref, own_ref, oth_ref, w_ref, q_ref, acc_ref, attn_ref, t0_ref, t1_ref, t2_ref, t3_ref, normed_ref, qf_ref, kf_ref, wbuf_ref, qbuf_ref, abuf_ref, k_ref, v_ref, sum_ref, turned_ref, sems):
    rows = own_ref.shape[0]
    half = rows // 2
    groups = wbuf_ref.shape[0]
    loads = []
    for g in range(groups):
        lanes = slice(g * GROUP, g * GROUP + GROUP)
        loads.append([
            pltpu.make_async_copy(w_ref.at[1:3, :, lanes], wbuf_ref.at[g], sems.at[g]),
            pltpu.make_async_copy(q_ref.at[g], qbuf_ref.at[g], sems.at[groups + g]),
            pltpu.make_async_copy(acc_ref.at[g], abuf_ref.at[g], sems.at[2 * groups + g]),
        ])
        for load in loads[-1]:
            load.start()
    norm_rows(place_ref[1], own_ref, oth_ref, normed_ref)
    qf_ref[...] = features(place_ref, place_ref[0] * rows, rows, BIG, -BIG)
    kf_ref[...] = features(place_ref, (1 - place_ref[0]) * rows, rows, 1.0, 1.0)
    ones = ones_block()
    near = pl.ds(pl.multiple_of(place_ref[0] * half, half), half)
    far = pl.ds(pl.multiple_of((1 - place_ref[0]) * half, half), half)
    low = lower_half(rows)
    for g in range(groups):
        for load in loads[g]:
            load.wait()
        normed = normed_ref[...]
        k_ref[...] = head_norm(jnp.dot(normed, wbuf_ref[g, 0], preferred_element_type=F32), ones).astype(BF)
        v_ref[...] = jnp.dot(normed, wbuf_ref[g, 1], preferred_element_type=F32).astype(BF)

        def emit_near(head, r):
            lanes = slice(head * 128, head * 128 + 128)
            sum_ref[:, lanes] = abuf_ref[g, :, lanes].astype(F32) + r

        def emit_far(head, r):
            lanes = slice(head * 128, head * 128 + 128)
            sum_ref[far, lanes] = sum_ref[far, lanes] + r

        attend_group(
            lambda lanes: qbuf_ref[g, :, lanes], lambda lanes: k_ref[near, lanes], lambda lanes: v_ref[near, lanes],
            qf_ref[...], kf_ref[near, :], emit_near,
        )
        attend_group(
            lambda lanes: qbuf_ref[g, far, lanes], lambda lanes: k_ref[far, lanes], lambda lanes: v_ref[far, lanes],
            qf_ref[far, :], kf_ref[far, :], emit_far,
        )
        for pair in range(2):
            even = sum_ref[:, pair * 256 : pair * 256 + 128]
            odd = sum_ref[:, pair * 256 + 128 : pair * 256 + 256]
            total = pltpu.roll(jnp.where(low, odd, even), HD, 1)
            first = g * GROUP + pair * 128
            attn = (jnp.where(low, even, odd) / total).astype(BF)
            attn_ref[:, first : first + 128] = attn
            turned_ref[first : first + 128, :] = attn.T
    for i, out in enumerate((t0_ref, t1_ref, t2_ref, t3_ref)):
        part = out.shape[0]
        out[...] = turned_ref[pl.ds(pl.multiple_of((i ^ place_ref[2]) * part, part), part), :]


def send_kernel(place_ref, attn_ref, w_ref, out_ref):
    out_ref[...] = jnp.dot(attn_ref[...], w_ref[...], preferred_element_type=F32).astype(BF)


def mixed_kernel(place_ref, attn_ref, w_ref, recv_ref, pick_ref, mixed_ref, send_ref, keep_ref):
    rows = attn_ref.shape[0]
    mixed = (jnp.dot(attn_ref[...], w_ref[...], preferred_element_type=F32) + recv_ref[...].astype(F32)).astype(BF)
    mixed_ref[...] = mixed
    row = lax.broadcasted_iota(jnp.int32, (rows, rows), 1)
    for half, out in ((0, send_ref), (1, keep_ref)):
        hot = jnp.where(pick_ref[half * rows : half * rows + rows, :] == row, 1.0, 0.0).astype(BF)
        out[...] = jnp.dot(hot, mixed, preferred_element_type=F32).astype(BF)


def call(kernel, place, grid, in_specs, out_specs, out_shape, scratch, flops, nbytes, args, alias=None, limit=VMEM_LIMIT):
    return pl.pallas_call(
        kernel,
        grid_spec=pltpu.PrefetchScalarGridSpec(
            num_scalar_prefetch=1, grid=grid, in_specs=in_specs, out_specs=out_specs, scratch_shapes=scratch
        ),
        out_shape=out_shape,
        input_output_aliases=alias or {},
        cost_estimate=pl.CostEstimate(flops=flops, bytes_accessed=nbytes, transcendentals=0),
        compiler_params=pltpu.CompilerParams(vmem_limit_bytes=limit),
    )(place, *args)


def whole(shape):
    return pl.BlockSpec(shape, lambda g, s: (0,) * len(shape))


def columns(rows, width):
    return pl.BlockSpec((rows, width), lambda g, s: (0, g))


def swap(value, axis):
    return lax.ppermute(value, axis, [(0, 1), (1, 0)])


def grad_kernel(place_ref, *refs):
    lefts, rights, outs, total_ref = refs[:4], refs[4:8], refs[8:12], refs[12]
    total = jnp.dot(lefts[0][...], rights[0][...], preferred_element_type=F32)
    for left, right in zip(lefts[1:], rights[1:]):
        total = total + jnp.dot(left[...], right[...], preferred_element_type=F32)
    total_ref[...] = total
    for i, out in enumerate(outs):
        piece = out.shape[0]
        out[...] = total_ref[pl.ds(pl.multiple_of((i ^ place_ref[3]) * piece, piece), piece), :].astype(BF)


def place_kernel(place_ref, *refs, count, scale):
    out_ref = refs[-1]
    for i in range(4):
        part_ref = refs[i * count // 4]
        of_each, piece, _ = part_ref.shape
        rows = pl.ds(pl.multiple_of((i ^ place_ref[3]) * piece, piece), piece)
        out_ref[rows, :] = part_ref[i % of_each].astype(F32) * scale


AXES = ("seq", "head", "z", "y", "xl")
ROUTES = (
    (("y", 0), ("y", 1), ("z", 0), ("z", 1)),
    (("z", 0), ("z", 1), ("y", 0), ("y", 1)),
)


def across(i, kind, n):
    if kind == 0:
        return i ^ 1
    return (i + 1) % n if i % 2 else (i - 1) % n


def bit_of(i, kind):
    return ((i + 1) >> 1) & 1 if kind == 0 else (i >> 1) & 1


def every_device(sizes):
    for i in range(sizes[0] * sizes[1] * sizes[2] * sizes[3] * sizes[4]):
        at, rest = {}, i
        for name, n in reversed(list(zip(AXES, sizes))):
            at[name] = rest % n
            rest //= n
        yield i, at


def index_of(at, sizes):
    i = 0
    for name, n in zip(AXES, sizes):
        i = i * n + at[name]
    return i


def pairs(sizes, partner):
    out = []
    for i, at in every_device(sizes):
        out.append((i, index_of(partner(at), sizes)))
    return out


def quad_tables(sizes, group):
    n = dict(zip(AXES, sizes))

    def partner(at, steps):
        for step in steps:
            axis, kind = ROUTES[at["head"]][2 * group + step]
            at = {**at, axis: across(at[axis], kind, n[axis])}
        return at

    return [pairs(sizes, lambda at, steps=steps: partner(at, steps)) for steps in ((1,), (0,), (0, 1))]


def x_tables(sizes):
    n = dict(zip(AXES, sizes))

    def partner(at, kinds):
        x = at["seq"] * n["xl"] + at["xl"]
        for kind in kinds:
            x = across(x, kind, n["seq"] * n["xl"])
        return {**at, "seq": x // n["xl"], "xl": x % n["xl"]}

    return [pairs(sizes, lambda at, kinds=kinds: partner(at, kinds)) for kinds in ((0,), (1,), (0, 1))]


def z_table(sizes):
    n = sizes[AXES.index("z")]
    return pairs(sizes, lambda at: {**at, "z": (at["z"] + n // 2) % n})


def mask_of(group, head):
    masks = []
    for core in (0, 1):
        mask = jnp.int32(0)
        for axis, kind in ROUTES[core][2 * group : 2 * group + 2]:
            mask = mask * 2 + bit_of(lax.axis_index(axis).astype(jnp.int32), kind)
        masks.append(mask)
    return jnp.where(head == 0, masks[0], masks[1])


def add(*terms):
    terms = [t.astype(F32) for t in terms]
    while len(terms) > 1:
        terms = [sum(terms[i + 1 : i + 2], terms[i]) for i in range(0, len(terms), 2)]
    return terms[0].astype(BF)


def move(value, table):
    return lax.ppermute(value, AXES, table)


def place_call(place, at, scale, parts, before):
    _, piece, width = parts[0].shape
    args, specs, alias = list(parts), [whole(part.shape) for part in parts], None
    if before is not None:
        args, specs, alias = args + [before], specs + [pl.BlockSpec(memory_space=pl.ANY)], {1 + len(parts): 0}
    return call(
        functools.partial(place_kernel, count=len(parts), scale=scale), place, (1,), specs,
        pl.BlockSpec((4 * piece, width), lambda g, s: (at ^ s[2], 0)),
        jax.ShapeDtypeStruct((16 * piece, width), F32), [], 10**6, 2 * 10**6, args, alias,
    )


def grad_call(place, lefts, rights):
    part, rows = lefts[0].shape
    width = rights[0].shape[1]
    piece = part // 4
    return call(
        grad_kernel, place, (width // GROUP,),
        [whole(lefts[0].shape)] * 4 + [columns(rows, GROUP)] * 4, [columns(piece, GROUP)] * 4,
        [jax.ShapeDtypeStruct((piece, width), BF)] * 4, [pltpu.VMEM((part, GROUP), F32)],
        12 * 10**8, 8 * 10**6, (*lefts, *rights), limit=BIG_VMEM,
    )


def body(tokens, lengths, owner_slot, latent_index, cotangent, qkv_weight, out_weight):
    own = tokens[0]
    rows, share = own.shape
    groups = share // GROUP
    seq = lax.axis_index("seq")
    head = lax.axis_index("head")
    sizes = lengths[0]
    place = jnp.concatenate([jnp.stack([seq, head, mask_of(0, head), mask_of(1, head)]).astype(jnp.int32), sizes])

    oth = swap(own, "head")
    foreign_own = swap(own, "seq")
    devices = tuple(lax.axis_size(a) for a in AXES)
    first, second = quad_tables(devices, 0), quad_tables(devices, 1)
    cots = [cotangent[0]] + [move(cotangent[0], table) for table in first]

    anywhere = pl.BlockSpec(memory_space=pl.ANY)
    scratch = lambda projections: [
        pltpu.VMEM((rows, 2 * share), BF),
        pltpu.VMEM((rows, 128), BF),
        pltpu.VMEM((rows, 128), BF),
        pltpu.VMEM((groups, projections, 2 * share, GROUP), BF),
        pltpu.VMEM((groups, rows, GROUP), BF),
        pltpu.VMEM((groups, rows, 2 * GROUP), BF),
        pltpu.VMEM((rows, GROUP), BF),
        pltpu.VMEM((rows, GROUP), BF),
    ]
    q, acc = call(
        local_kernel, place, (1,), [whole((rows, share)), whole((rows, share)), anywhere], [anywhere] * 2,
        [jax.ShapeDtypeStruct((groups, rows, GROUP), BF), jax.ShapeDtypeStruct((groups, rows, 2 * GROUP), BF)],
        scratch(3) + [pltpu.SemaphoreType.DMA((3 * groups,))], 10**8, 10**6, (own, oth, qkv_weight), limit=BIG_VMEM,
    )
    foreign_own, q, cots[1], cots[2] = lax.optimization_barrier((foreign_own, q, cots[1], cots[2]))
    foreign_oth = swap(foreign_own, "head")
    quarter = whole((share // 4, rows))
    attn, *turned = call(
        foreign_kernel, place, (1,), [whole((rows, share)), whole((rows, share))] + [anywhere] * 3,
        [whole((rows, share))] + [quarter] * 4,
        [jax.ShapeDtypeStruct((rows, share), BF)] + [jax.ShapeDtypeStruct((share // 4, rows), BF)] * 4,
        scratch(2)
        + [pltpu.VMEM((rows, 2 * GROUP), F32), pltpu.VMEM((share, rows), BF), pltpu.SemaphoreType.DMA((3 * groups,))],
        10**9, 10**6, (foreign_own, foreign_oth, qkv_weight, q, acc), limit=BIG_VMEM,
    )
    attn, latent_index, sizes, owner_slot = lax.optimization_barrier((attn, latent_index, sizes, owner_slot))
    ends = jnp.cumsum(sizes, dtype=jnp.int32)
    starts = ends - sizes
    slots = owner_slot[0]
    picks = starts[:, None] + jnp.remainder(latent_index[0], sizes[:, None])
    order = slots[None, :] == jnp.arange(IMAGES, dtype=jnp.int32)[:, None]
    by_slot = jnp.sum(jnp.where(order[:, :, None], picks[None], 0), axis=1).reshape(2, rows)
    local = by_slot - seq * rows
    local = jnp.stack([jnp.where(seq == 0, local[1], local[0]), jnp.where(seq == 0, local[0], local[1])])
    local = local.reshape(2 * rows, 1)

    lefts = [turned[0]] + [move(t, table) for t, table in zip(turned[1:], first)]

    pieces = list(grad_call(place, lefts, cots))
    pieces[0], attn = lax.optimization_barrier((pieces[0], attn))
    away = [move(p, table) for p, table in zip(pieces[1:], second)]
    partial = call(
        send_kernel, place, (groups,),
        [whole((rows, share)), pl.BlockSpec((share, GROUP), lambda g, s: (0, (1 - s[1]) * groups + g))],
        columns(rows, GROUP), jax.ShapeDtypeStruct((rows, share), BF), [], 6 * 10**8, 3 * 10**6, (attn, out_weight), limit=BIG_VMEM,
    )
    away[2], partial = lax.optimization_barrier((away[2], partial))
    grad = add(pieces[0], *away)
    recv = swap(partial, "head")
    over_x = [move(grad, table) for table in x_tables(devices)]
    over_x[2], local = lax.optimization_barrier((over_x[2], local))
    grad, attn = lax.optimization_barrier((add(grad, *over_x), attn))
    over_z = move(grad, z_table(devices))
    shape = jax.ShapeDtypeStruct((rows, share), BF)
    mixed, send, keep = call(
        mixed_kernel, place, (groups,),
        [whole((rows, share)), pl.BlockSpec((share, GROUP), lambda g, s: (0, s[1] * groups + g)),
         columns(rows, GROUP), whole((2 * rows, 1))],
        [columns(rows, GROUP)] * 3, [shape] * 3, [], 14 * 10**8, 6 * 10**6, (attn, out_weight, recv, local),
    )
    over_z, send = lax.optimization_barrier((over_z, send))
    grad = add(grad, over_z)
    latents = keep + swap(send, "seq")
    held = jnp.stack([grad] + [move(grad, table) for table in second])
    across_one, across_zero = move(held, first[0]), move(held, first[1])
    scale = (2 * rows * lax.axis_size("z") * lax.axis_size("y") * lax.axis_size("xl")) ** (-0.5)
    grad_out = place_call(place, 0, scale, [held], None)
    across_one, grad_out = lax.optimization_barrier((across_one, grad_out))
    fourth = [move(across_one[:2], first[1]), move(across_zero[2:], first[0])]
    grad_out = place_call(place, 1, scale, [across_one], grad_out)
    grad_out = place_call(place, 2, scale, [across_zero], grad_out)
    grad_out = place_call(place, 3, scale, fourth, grad_out)
    return mixed[None], latents[None], grad_out


def on_mesh(fine):
    dp = ("z", "y", "xl")
    in_specs = (
        P(dp, "seq", "head"),
        P(dp, None),
        P(dp, None),
        P(dp, None, None),
        P(dp, "seq", None),
        P(None, None, "head"),
        P("head", None),
    )
    out_specs = (P(dp, "seq", "head"), P(dp, "seq", "head"), P("head", None))
    return jax.shard_map(body, mesh=fine, in_specs=in_specs, out_specs=out_specs, check_vma=False)


def solution(mesh):
    return on_mesh(Mesh(mesh.devices.reshape(2, 2, 8, 4, 2), ("seq", "head", "z", "y", "xl")))
```

profile of v0, /device:TPU:2, one launch (start us, length us, event | category | flops | bytes accessed | tf_op | source)
XLA Modules:
  0.0 126.9 jit_solution(16746770060690732603)
XLA Ops:
  0.6 1.7 %collective-permute-start.3 = (bf16[512,1536]{1,0:T(8,128)(2,1)}, bf16[512,1536]{1,0:T(8,128)(2,1)S(1)}, u32[]{:S(2)}, u32[]{:S(2)}) collective-permute-start(bf16[512,1536]{1,0:T(8,128)(2,1)} %bitcast.27), channel_id=1, source_target_pairs={{0,2},{1,3},{2,0},{3,1},{4,6},{5,7},{6,4},{7,5},{8,10},{9,11},{10,... | collective-permute-start | bytes 4718600 | tf_op jit(solution)/shard_map/ppermute | solution.py:340
  2.3 2.2 %collective-permute-start.2 = (bf16[512,1536]{1,0:T(8,128)(2,1)}, bf16[512,1536]{1,0:T(8,128)(2,1)}, u32[]{:S(2)}, u32[]{:S(2)}) collective-permute-start(bf16[512,1536]{1,0:T(8,128)(2,1)} %bitcast.28), channel_id=1, source_target_pairs={{0,6},{1,7},{2,4},{3,5},{4,2},{5,3},{6,0},{7,1},{8,14},{9,15},{10,... | collective-permute-start | bytes 4718600 | tf_op jit(solution)/shard_map/ppermute | solution.py:340
  4.5 2.4 %collective-permute-start.1 = (bf16[512,768]{1,0:T(8,128)(2,1)}, bf16[512,768]{1,0:T(8,128)(2,1)}, u32[]{:S(2)}, u32[]{:S(2)}) collective-permute-start(bf16[512,768]{1,0:T(8,128)(2,1)} %bitcast.31), channel_id=1, source_target_pairs={{0,64},{64,0},{1,65},{65,1},{2,66},{66,2},{3,67},{67,3},{4,68},{68... | collective-permute-start | bytes 2359304 | tf_op jit(solution)/shard_map/ppermute | solution.py:230
  6.9 2.1 %collective-permute-start = (bf16[512,768]{1,0:T(8,128)(2,1)}, bf16[512,768]{1,0:T(8,128)(2,1)}, u32[]{:S(2)}, u32[]{:S(2)}) collective-permute-start(bf16[512,768]{1,0:T(8,128)(2,1)} %bitcast.32), channel_id=1, source_target_pairs={{0,128},{128,0},{1,129},{129,1},{2,130},{130,2},{3,131},{131,3},{4... | collective-permute-start | bytes 2359304 | tf_op jit(solution)/shard_map/ppermute | solution.py:230
  9.0 1.3 %concatenate.3.place_ref = s32[12]{0:T(128)} concatenate(s32[1]{0:T(128)} %bitcast, s32[1]{0:T(128)} %bitcast.1, s32[1]{0:T(128)} %bitcast.2, s32[1]{0:T(128)} %bitcast.3, s32[8]{0:T(128)} %bitcast.41), dimensions={0} | concatenate | bytes 96 | tf_op jit(solution)/shard_map/concatenate | solution.py:374
  10.3 17.6 %shard_map.94 = (bf16[3,512,256]{2,1,0:T(8,128)(2,1)}, bf16[3,512,512]{2,1,0:T(8,128)(2,1)}) custom-call(s32[12]{0:T(128)} %concatenate.3.place_ref, bf16[512,768]{1,0:T(8,128)(2,1)} %bitcast.33, bf16[512,768]{1,0:T(8,128)(2,1)} %collective-permute-done.1.oth_ref, bf16[3,1536,768]{2,1,0:T(8,128)(2,1)} %w_ref.5), custom_call_target="tpu_custom_call" | custom-call | flops 100000000 | bytes 1000000 | tf_op jit(solution)/shard_map/pallas_call | solution.py:209
  27.9 0.2 collective-permute-done.own_ref
  28.2 3.5 %collective-permute-start.8 = (bf16[512,1536]{1,0:T(8,128)(2,1)S(1)}, bf16[512,1536]{1,0:T(8,128)(2,1)}, u32[]{:S(2)}, u32[]{:S(2)}) collective-permute-start(bf16[512,1536]{1,0:T(8,128)(2,1)S(1)} %bitcast.30), channel_id=1, source_target_pairs={{0,4},{1,5},{2,6},{3,7},{4,0},{5,1},{6,2},{7,3},{8,12},{9,13},{10,... | collective-permute-start | bytes 4718600 | tf_op jit(solution)/shard_map/ppermute | solution.py:340
  31.7 15.4 %shard_map.95 = (bf16[512,768]{1,0:T(8,128)(2,1)}, bf16[192,512]{1,0:T(8,128)(2,1)}, bf16[192,512]{1,0:T(8,128)(2,1)}, bf16[192,512]{1,0:T(8,128)(2,1)}, bf16[192,512]{1,0:T(8,128)(2,1)}) custom-call(s32[12]{0:T(128)} %concatenate.3.place_ref, bf16[512,768]{1,0:T(8,128)(2,1)} %collective-permute-done.own_ref, ...), custom_call_target="tpu_custom_call" | custom-call | flops 1000000000 | bytes 1000000 | tf_op jit(solution)/shard_map/pallas_call | solution.py:209
  47.3 2.2 %collective-permute-start.5 = (bf16[192,512]{1,0:T(8,128)(2,1)}, bf16[192,512]{1,0:T(8,128)(2,1)S(1)}, u32[]{:S(2)}, u32[]{:S(2)}) collective-permute-start(bf16[192,512]{1,0:T(8,128)(2,1)} %get-tuple-element.42), channel_id=1, source_target_pairs={{0,6},{1,7},{2,4},{3,5},{4,2},{5,3},{6,0},{7,1},{8,14},{9,15},{10,... | collective-permute-start | bytes 589832 | tf_op jit(solution)/shard_map/ppermute | solution.py:340
  49.7 2.4 %collective-permute-start.7 = (bf16[192,512]{1,0:T(8,128)(2,1)}, bf16[192,512]{1,0:T(8,128)(2,1)S(1)}, u32[]{:S(2)}, u32[]{:S(2)}) collective-permute-start(bf16[192,512]{1,0:T(8,128)(2,1)} %get-tuple-element.44), channel_id=1, source_target_pairs={{0,4},{1,5},{2,6},{3,7},{4,0},{5,1},{6,2},{7,3},{8,12},{9,13},{10,... | collective-permute-start | bytes 589832 | tf_op jit(solution)/shard_map/ppermute | solution.py:340
  52.4 2.0 %collective-permute-done.5.refs_1_ = bf16[192,512]{1,0:T(8,128)(2,1)S(1)} collective-permute-done((bf16[192,512]{1,0:T(8,128)(2,1)}, bf16[192,512]{1,0:T(8,128)(2,1)S(1)}, u32[]{:S(2)}, u32[]{:S(2)}) %collective-permute-start.5) | collective-permute-done | bytes 196640 | tf_op jit(solution)/shard_map/ppermute | solution.py:340
  54.4 1.0 collective-permute-done.6.refs_2_
  55.4 2.6 %collective-permute-done.7.refs_3_ = bf16[192,512]{1,0:T(8,128)(2,1)S(1)} collective-permute-done((bf16[192,512]{1,0:T(8,128)(2,1)}, bf16[192,512]{1,0:T(8,128)(2,1)S(1)}, u32[]{:S(2)}, u32[]{:S(2)}) %collective-permute-start.7) | collective-permute-done | bytes 196640 | tf_op jit(solution)/shard_map/ppermute | solution.py:340
  58.0 0.7 copy-done.8
  58.7 7.3 %shard_map.96 = (bf16[48,1536]{1,0:T(8,128)(2,1)}, bf16[48,1536]{1,0:T(8,128)(2,1)}, bf16[48,1536]{1,0:T(8,128)(2,1)}, bf16[48,1536]{1,0:T(8,128)(2,1)}) custom-call(s32[12]{0:T(128)} %concatenate.3.place_ref, bf16[192,512]{1,0:T(8,128)(2,1)} %get-tuple-element.41.refs_0_, bf16[192,512]{1,0:T(8,128)(2,1)} %copy-done.6, bf16[192,512]{1,0:T(8,128)(2,1)} %copy-done.7, ...), custom_call_target="tpu_custom_call" | custom-call | flops 1200000000 | bytes 8000000 | tf_op jit(solution)/shard_map/pallas_call | solution.py:209
  66.0 3.2 %collective-permute-start.9 = (bf16[48,1536]{1,0:T(8,128)(2,1)}, bf16[48,1536]{1,0:T(8,128)(2,1)S(1)}, u32[]{:S(2)}, u32[]{:S(2)}) collective-permute-start(bf16[48,1536]{1,0:T(8,128)(2,1)} %get-tuple-element.51), channel_id=1, source_target_pairs={{0,56},{1,57},{2,58},{3,59},{4,60},{5,61},{6,62},{7,63},{8,16},{9,... | collective-permute-start | bytes 442376 | tf_op jit(solution)/shard_map/ppermute | solution.py:340
  69.2 2.5 %collective-permute-start.11 = (bf16[48,1536]{1,0:T(8,128)(2,1)}, bf16[48,1536]{1,0:T(8,128)(2,1)S(1)}, u32[]{:S(2)}, u32[]{:S(2)}) collective-permute-start(bf16[48,1536]{1,0:T(8,128)(2,1)} %get-tuple-element.53), channel_id=1, source_target_pairs={{0,16},{1,17},{2,18},{3,19},{4,20},{5,21},{6,22},{7,23},{8,56},{9,... | collective-permute-start | bytes 442376 | tf_op jit(solution)/shard_map/ppermute | solution.py:340
  71.6 4.8 %shard_map.97 = bf16[512,768]{1,0:T(8,128)(2,1)} custom-call(s32[12]{0:T(128)} %concatenate.3.place_ref, bf16[512,768]{1,0:T(8,128)(2,1)} %get-tuple-element.60.attn_ref, bf16[768,1536]{1,0:T(8,128)(2,1)} %w_ref.7), custom_call_target="tpu_custom_call" | custom-call | flops 600000000 | bytes 3000000 | tf_op jit(solution)/shard_map/pallas_call | solution.py:209
  76.4 0.2 collective-permute-done.11
  76.7 2.2 %collective-permute-start.14 = (bf16[48,1536]{1,0:T(8,128)(2,1)S(1)}, bf16[48,1536]{1,0:T(8,128)(2,1)S(1)}, u32[]{:S(2)}, u32[]{:S(2)}) collective-permute-start(bf16[48,1536]{1,0:T(8,128)(2,1)S(1)} %add_convert_fusion.2), channel_id=1, source_target_pairs={{0,128},{1,129},{2,130},{3,131},{4,132},{5,133},{6,134},{7,135},{8... | collective-permute-start | bytes 442376 | tf_op jit(solution)/shard_map/ppermute | solution.py:340
  79.0 2.5 %collective-permute-start.12 = (bf16[48,1536]{1,0:T(8,128)(2,1)S(1)}, bf16[48,1536]{1,0:T(8,128)(2,1)S(1)}, u32[]{:S(2)}, u32[]{:S(2)}) collective-permute-start(bf16[48,1536]{1,0:T(8,128)(2,1)S(1)} %add_convert_fusion.2), channel_id=1, source_target_pairs={{0,1},{1,0},{2,3},{3,2},{4,5},{5,4},{6,7},{7,6},{8,9},{9,8},{10,11... | collective-permute-start | bytes 442376 | tf_op jit(solution)/shard_map/ppermute | solution.py:340
  81.5 2.0 %collective-permute-done.14 = bf16[48,1536]{1,0:T(8,128)(2,1)S(1)} collective-permute-done((bf16[48,1536]{1,0:T(8,128)(2,1)S(1)}, bf16[48,1536]{1,0:T(8,128)(2,1)S(1)}, u32[]{:S(2)}, u32[]{:S(2)}) %collective-permute-start.14) | collective-permute-done | bytes 147488 | tf_op jit(solution)/shard_map/ppermute | solution.py:340
  83.6 1.5 %collective-permute-done.13 = bf16[48,1536]{1,0:T(8,128)(2,1)S(1)} collective-permute-done((bf16[48,1536]{1,0:T(8,128)(2,1)S(1)}, bf16[48,1536]{1,0:T(8,128)(2,1)S(1)}, u32[]{:S(2)}, u32[]{:S(2)}) %collective-permute-start.13) | collective-permute-done | bytes 147488 | tf_op jit(solution)/shard_map/ppermute | solution.py:340
  85.2 3.8 %collective-permute-start.16 = (bf16[48,1536]{1,0:T(8,128)(2,1)S(1)}, bf16[48,1536]{1,0:T(8,128)(2,1)S(1)}, u32[]{:S(2)}, u32[]{:S(2)}) collective-permute-start(bf16[48,1536]{1,0:T(8,128)(2,1)S(1)} %add_convert_fusion.1), channel_id=1, source_target_pairs={{0,32},{1,33},{2,34},{3,35},{4,36},{5,37},{6,38},{7,39},{8,40},{9,... | collective-permute-start | bytes 442376 | tf_op jit(solution)/shard_map/ppermute | solution.py:340
  89.0 1.0 copy.14.pick_ref
  90.1 1.0 copy-done.2
  91.1 5.1 %shard_map.98 = (bf16[512,768]{1,0:T(8,128)(2,1)}, bf16[512,768]{1,0:T(8,128)(2,1)S(1)}, bf16[512,768]{1,0:T(8,128)(2,1)S(1)}) custom-call(s32[12]{0:T(128)S(1)} %copy-done.3, bf16[512,768]{1,0:T(8,128)(2,1)S(1)} %copy-done.1, bf16[768,1536]{1,0:T(8,128)(2,1)S(1)} %copy-done, bf16[512,768]{1,0:T(8,128)(2,1)} %collective-permute-done.15.recv_ref, ...), custom_call_target="tpu_custom_call" | custom-call | flops 1400000000 | bytes 6000000 | tf_op jit(solution)/shard_map/pallas_call | solution.py:209
  96.3 1.3 collective-permute-start.20
  97.6 1.7 %collective-permute-start.19 = (bf16[48,1536]{1,0:T(8,128)(2,1)S(1)}, bf16[48,1536]{1,0:T(8,128)(2,1)S(1)}, u32[]{:S(2)}, u32[]{:S(2)}) collective-permute-start(bf16[48,1536]{1,0:T(8,128)(2,1)S(1)} %add_convert_fusion), channel_id=1, source_target_pairs={{0,8},{1,9},{2,10},{3,11},{4,12},{5,13},{6,14},{7,15},{8,0},{9,1},... | collective-permute-start | bytes 442376 | tf_op jit(solution)/shard_map/ppermute | solution.py:340
  99.2 1.8 %collective-permute-start.18 = (bf16[48,1536]{1,0:T(8,128)(2,1)S(1)}, bf16[48,1536]{1,0:T(8,128)(2,1)S(1)}, u32[]{:S(2)}, u32[]{:S(2)}) collective-permute-start(bf16[48,1536]{1,0:T(8,128)(2,1)S(1)} %add_convert_fusion), channel_id=1, source_target_pairs={{0,56},{1,57},{2,58},{3,59},{4,60},{5,61},{6,62},{7,63},{8,16},{9,... | collective-permute-start | bytes 442376 | tf_op jit(solution)/shard_map/ppermute | solution.py:340
  101.1 2.3 %collective-permute-start.17 = (bf16[512,768]{1,0:T(8,128)(2,1)S(1)}, bf16[512,768]{1,0:T(8,128)(2,1)S(1)}, u32[]{:S(2)}, u32[]{:S(2)}) collective-permute-start(bf16[512,768]{1,0:T(8,128)(2,1)S(1)} %get-tuple-element.67), channel_id=1, source_target_pairs={{0,128},{128,0},{1,129},{129,1},{2,130},{130,2},{3,131},{131,3},{4... | collective-permute-start | bytes 2359304 | tf_op jit(solution)/shard_map/ppermute | solution.py:230
  103.4 0.2 collective-permute-done.20
  103.6 1.1 collective-permute-done.19
  104.7 2.2 %collective-permute-done.18 = bf16[48,1536]{1,0:T(8,128)(2,1)S(1)} collective-permute-done((bf16[48,1536]{1,0:T(8,128)(2,1)S(1)}, bf16[48,1536]{1,0:T(8,128)(2,1)S(1)}, u32[]{:S(2)}, u32[]{:S(2)}) %collective-permute-start.18) | collective-permute-done | bytes 147488 | tf_op jit(solution)/shard_map/ppermute | solution.py:340
  107.0 0.3 collective-permute-start.23
  107.3 1.9 %collective-permute-start.21 = (bf16[4,48,1536]{2,1,0:T(8,128)(2,1)S(1)}, bf16[4,48,1536]{2,1,0:T(8,128)(2,1)S(1)}, u32[]{:S(2)}, u32[]{:S(2)}) collective-permute-start(bf16[4,48,1536]{2,1,0:T(8,128)(2,1)S(1)} %pad_maximum_fusion.refs_0_), channel_id=1, source_target_pairs={{0,6},{1,7},{2,4},{3,5},{4,2},{5,3},{6,0},{7,1},{8,14},{9,15},{10,... | collective-permute-start | bytes 1769480 | tf_op jit(solution)/shard_map/ppermute | solution.py:340
  109.2 1.6 %shard_map.99.refs_1_ = f32[768,1536]{1,0:T(8,128)} custom-call(s32[12]{0:T(128)S(1)} %copy-done.3, bf16[4,48,1536]{2,1,0:T(8,128)(2,1)S(1)} %pad_maximum_fusion.refs_0_), custom_call_target="tpu_custom_call" | custom-call | flops 1000000 | bytes 2000000 | tf_op jit(solution)/shard_map/pallas_call | solution.py:209
  110.8 6.1 %collective-permute-done.23.refs_0_ = bf16[4,48,1536]{2,1,0:T(8,128)(2,1)S(1)} collective-permute-done((bf16[4,48,1536]{2,1,0:T(8,128)(2,1)S(1)}, bf16[4,48,1536]{2,1,0:T(8,128)(2,1)S(1)}, u32[]{:S(2)}, u32[]{:S(2)}) %collective-permute-start.23) | collective-permute-done | bytes 589856 | tf_op jit(solution)/shard_map/ppermute | solution.py:340
  117.0 0.2 collective-permute-start.24
  117.2 1.3 collective-permute-done.21.refs_0_
  118.5 0.6 collective-permute-start.22
  119.1 1.6 %shard_map.100.refs_1_ = f32[768,1536]{1,0:T(8,128)} custom-call(s32[12]{0:T(128)S(1)} %copy-done.3, bf16[4,48,1536]{2,1,0:T(8,128)(2,1)S(1)} %collective-permute-done.21.refs_0_, f32[768,1536]{1,0:T(8,128)} %shard_map.99.refs_1_), custom_call_target="tpu_custom_call", output_to_operand_aliasing={{}: (2, {})} | custom-call | flops 1000000 | bytes 2000000 | tf_op jit(solution)/shard_map/pallas_call | solution.py:209
  120.7 1.6 %shard_map.101.refs_2_ = f32[768,1536]{1,0:T(8,128)} custom-call(s32[12]{0:T(128)S(1)} %copy-done.3, bf16[4,48,1536]{2,1,0:T(8,128)(2,1)S(1)} %collective-permute-done.23.refs_0_, f32[768,1536]{1,0:T(8,128)} %shard_map.100.refs_1_), custom_call_target="tpu_custom_call", output_to_operand_aliasing={{}: (2, {})} | custom-call | flops 1000000 | bytes 2000000 | tf_op jit(solution)/shard_map/pallas_call | solution.py:209
  122.4 1.0 add_bitcast_fusion
  123.3 1.7 %collective-permute-done.24.refs_1_ = bf16[2,48,1536]{2,1,0:T(8,128)(2,1)S(1)} collective-permute-done((bf16[2,48,1536]{2,1,0:T(8,128)(2,1)S(1)}, bf16[2,48,1536]{2,1,0:T(8,128)(2,1)S(1)}, u32[]{:S(2)}, u32[]{:S(2)}) %collective-permute-start.24) | collective-permute-done | bytes 294944 | tf_op jit(solution)/shard_map/ppermute | solution.py:340
  125.0 0.3 collective-permute-done.22.refs_0_
  125.3 1.6 %shard_map.102 = f32[768,1536]{1,0:T(8,128)} custom-call(s32[12]{0:T(128)S(1)} %copy-done.3, bf16[2,48,1536]{2,1,0:T(8,128)(2,1)S(1)} %collective-permute-done.22.refs_0_, bf16[2,48,1536]{2,1,0:T(8,128)(2,1)S(1)} %collective-permute-done.24.refs_1_, f32[768,1536]{1,0:T(8,128)} %shard_map.101.refs_2_), custom_call_target="tpu_custom_call", output_to_operand_aliasing={{}: (3, {})} | custom-call | flops 1000000 | bytes 2000000 | tf_op jit(solution)/shard_map/pallas_call | solution.py:209
  (56 shorter events, 1.3 us)
Async XLA Ops:
  0.6 27.5 %collective-permute-start.3 = (bf16[512,1536]{1,0:T(8,128)(2,1)}, bf16[512,1536]{1,0:T(8,128)(2,1)S(1)}, u32[]{:S(2)}, u32[]{:S(2)}) collective-permute-start(bf16[512,1536]{1,0:T(8,128)(2,1)} %bitcast.27), channel_id=1, source_target_pairs={{0,2},{1,3},{2,0},{3,1},{4,6},{5,7},{6,4},{7,5},{8,10},{9,11},{10,... | collective-permute-start | bytes 4718600 | tf_op jit(solution)/shard_map/ppermute | solution.py:340
  2.3 25.8 %collective-permute-start.2 = (bf16[512,1536]{1,0:T(8,128)(2,1)}, bf16[512,1536]{1,0:T(8,128)(2,1)}, u32[]{:S(2)}, u32[]{:S(2)}) collective-permute-start(bf16[512,1536]{1,0:T(8,128)(2,1)} %bitcast.28), channel_id=1, source_target_pairs={{0,6},{1,7},{2,4},{3,5},{4,2},{5,3},{6,0},{7,1},{8,14},{9,15},{10,... | collective-permute-start | bytes 4718600 | tf_op jit(solution)/shard_map/ppermute | solution.py:340
  4.5 5.8 %collective-permute-start.1 = (bf16[512,768]{1,0:T(8,128)(2,1)}, bf16[512,768]{1,0:T(8,128)(2,1)}, u32[]{:S(2)}, u32[]{:S(2)}) collective-permute-start(bf16[512,768]{1,0:T(8,128)(2,1)} %bitcast.31), channel_id=1, source_target_pairs={{0,64},{64,0},{1,65},{65,1},{2,66},{66,2},{3,67},{67,3},{4,68},{68... | collective-permute-start | bytes 2359304 | tf_op jit(solution)/shard_map/ppermute | solution.py:230
  6.9 21.3 %collective-permute-start = (bf16[512,768]{1,0:T(8,128)(2,1)}, bf16[512,768]{1,0:T(8,128)(2,1)}, u32[]{:S(2)}, u32[]{:S(2)}) collective-permute-start(bf16[512,768]{1,0:T(8,128)(2,1)} %bitcast.32), channel_id=1, source_target_pairs={{0,128},{128,0},{1,129},{129,1},{2,130},{130,2},{3,131},{131,3},{4... | collective-permute-start | bytes 2359304 | tf_op jit(solution)/shard_map/ppermute | solution.py:230
  10.3 17.9 %copy-start.4 = (bf16[1,512,1536]{2,1,0:T(8,128)(2,1)S(1)}, bf16[1,512,1536]{2,1,0:T(8,128)(2,1)}, u32[]{:S(2)}) copy-start(bf16[1,512,1536]{2,1,0:T(8,128)(2,1)} %param.11) | copy-start | bytes 4718596
  28.1 19.0 %copy-start.5 = (bf16[512,1536]{1,0:T(8,128)(2,1)}, bf16[512,1536]{1,0:T(8,128)(2,1)S(1)}, u32[]{:S(2)}) copy-start(bf16[512,1536]{1,0:T(8,128)(2,1)S(1)} %collective-permute-done.3.refs_6_) | copy-start | bytes 4718596
  28.1 3.6 %collective-permute-start.4 = (bf16[512,768]{1,0:T(8,128)(2,1)}, bf16[512,768]{1,0:T(8,128)(2,1)}, u32[]{:S(2)}, u32[]{:S(2)}) collective-permute-start(bf16[512,768]{1,0:T(8,128)(2,1)} %collective-permute-done.own_ref), channel_id=1, source_target_pairs={{0,64},{64,0},{1,65},{65,1},{2,66},{66,2},{3,67},{67,3},{4,68},{68... | collective-permute-start | bytes 2359304 | tf_op jit(solution)/shard_map/ppermute | solution.py:230
  28.2 24.1 %collective-permute-start.8 = (bf16[512,1536]{1,0:T(8,128)(2,1)S(1)}, bf16[512,1536]{1,0:T(8,128)(2,1)}, u32[]{:S(2)}, u32[]{:S(2)}) collective-permute-start(bf16[512,1536]{1,0:T(8,128)(2,1)S(1)} %bitcast.30), channel_id=1, source_target_pairs={{0,4},{1,5},{2,6},{3,7},{4,0},{5,1},{6,2},{7,3},{8,12},{9,13},{10,... | collective-permute-start | bytes 4718600 | tf_op jit(solution)/shard_map/ppermute | solution.py:340
  31.7 15.4 %copy-start.11 = (s32[1,8]{1,0:T(1,128)S(1)}, s32[1,8]{1,0:T(1,128)}, u32[]{:S(2)}) copy-start(s32[1,8]{1,0:T(1,128)} %param.8) | copy-start | bytes 100
  31.7 20.4 %copy-start.10 = (s32[1,8,128]{2,1,0:T(8,128)S(1)}, s32[1,8,128]{2,1,0:T(8,128)}, u32[]{:S(2)}) copy-start(s32[1,8,128]{2,1,0:T(8,128)} %param.10) | copy-start | bytes 12292
  31.7 20.6 %copy-start.12 = (s32[1,8]{1,0:T(1,128)S(1)}, s32[1,8]{1,0:T(1,128)}, u32[]{:S(2)}) copy-start(s32[1,8]{1,0:T(1,128)} %param.9) | copy-start | bytes 100
  47.3 7.1 %collective-permute-start.5 = (bf16[192,512]{1,0:T(8,128)(2,1)}, bf16[192,512]{1,0:T(8,128)(2,1)S(1)}, u32[]{:S(2)}, u32[]{:S(2)}) collective-permute-start(bf16[192,512]{1,0:T(8,128)(2,1)} %get-tuple-element.42), channel_id=1, source_target_pairs={{0,6},{1,7},{2,4},{3,5},{4,2},{5,3},{6,0},{7,1},{8,14},{9,15},{10,... | collective-permute-start | bytes 589832 | tf_op jit(solution)/shard_map/ppermute | solution.py:340
  49.5 5.9 %collective-permute-start.6 = (bf16[192,512]{1,0:T(8,128)(2,1)}, bf16[192,512]{1,0:T(8,128)(2,1)S(1)}, u32[]{:S(2)}, u32[]{:S(2)}) collective-permute-start(bf16[192,512]{1,0:T(8,128)(2,1)} %get-tuple-element.43), channel_id=1, source_target_pairs={{0,2},{1,3},{2,0},{3,1},{4,6},{5,7},{6,4},{7,5},{8,10},{9,11},{10,... | collective-permute-start | bytes 589832 | tf_op jit(solution)/shard_map/ppermute | solution.py:340
  49.7 8.4 %collective-permute-start.7 = (bf16[192,512]{1,0:T(8,128)(2,1)}, bf16[192,512]{1,0:T(8,128)(2,1)S(1)}, u32[]{:S(2)}, u32[]{:S(2)}) collective-permute-start(bf16[192,512]{1,0:T(8,128)(2,1)} %get-tuple-element.44), channel_id=1, source_target_pairs={{0,4},{1,5},{2,6},{3,7},{4,0},{5,1},{6,2},{7,3},{8,12},{9,13},{10,... | collective-permute-start | bytes 589832 | tf_op jit(solution)/shard_map/ppermute | solution.py:340
  54.4 3.6 %copy-start.6 = (bf16[192,512]{1,0:T(8,128)(2,1)}, bf16[192,512]{1,0:T(8,128)(2,1)S(1)}, u32[]{:S(2)}) copy-start(bf16[192,512]{1,0:T(8,128)(2,1)S(1)} %collective-permute-done.5.refs_1_) | copy-start | bytes 589828
  55.4 2.6 %copy-start.7 = (bf16[192,512]{1,0:T(8,128)(2,1)}, bf16[192,512]{1,0:T(8,128)(2,1)S(1)}, u32[]{:S(2)}) copy-start(bf16[192,512]{1,0:T(8,128)(2,1)S(1)} %collective-permute-done.6.refs_2_) | copy-start | bytes 589828
  58.0 0.7 copy-start.8
  66.0 10.7 %copy-start.9 = (bf16[48,1536]{1,0:T(8,128)(2,1)S(1)}, bf16[48,1536]{1,0:T(8,128)(2,1)}, u32[]{:S(2)}) copy-start(bf16[48,1536]{1,0:T(8,128)(2,1)} %get-tuple-element.50) | copy-start | bytes 442372
  66.0 10.7 %collective-permute-start.9 = (bf16[48,1536]{1,0:T(8,128)(2,1)}, bf16[48,1536]{1,0:T(8,128)(2,1)S(1)}, u32[]{:S(2)}, u32[]{:S(2)}) collective-permute-start(bf16[48,1536]{1,0:T(8,128)(2,1)} %get-tuple-element.51), channel_id=1, source_target_pairs={{0,56},{1,57},{2,58},{3,59},{4,60},{5,61},{6,62},{7,63},{8,16},{9,... | collective-permute-start | bytes 442376 | tf_op jit(solution)/shard_map/ppermute | solution.py:340
  69.2 7.5 %collective-permute-start.10 = (bf16[48,1536]{1,0:T(8,128)(2,1)}, bf16[48,1536]{1,0:T(8,128)(2,1)S(1)}, u32[]{:S(2)}, u32[]{:S(2)}) collective-permute-start(bf16[48,1536]{1,0:T(8,128)(2,1)} %get-tuple-element.52), channel_id=1, source_target_pairs={{0,8},{1,9},{2,10},{3,11},{4,12},{5,13},{6,14},{7,15},{8,0},{9,1},... | collective-permute-start | bytes 442376 | tf_op jit(solution)/shard_map/ppermute | solution.py:340
  69.2 7.5 %collective-permute-start.11 = (bf16[48,1536]{1,0:T(8,128)(2,1)}, bf16[48,1536]{1,0:T(8,128)(2,1)S(1)}, u32[]{:S(2)}, u32[]{:S(2)}) collective-permute-start(bf16[48,1536]{1,0:T(8,128)(2,1)} %get-tuple-element.53), channel_id=1, source_target_pairs={{0,16},{1,17},{2,18},{3,19},{4,20},{5,21},{6,22},{7,23},{8,56},{9,... | collective-permute-start | bytes 442376 | tf_op jit(solution)/shard_map/ppermute | solution.py:340
  71.6 18.4 %copy-start = (bf16[768,1536]{1,0:T(8,128)(2,1)S(1)}, bf16[768,1536]{1,0:T(8,128)(2,1)}, u32[]{:S(2)}) copy-start(bf16[768,1536]{1,0:T(8,128)(2,1)} %w_ref.7) | copy-start | bytes 7077892
  71.6 18.4 %copy-start.1 = (bf16[512,768]{1,0:T(8,128)(2,1)S(1)}, bf16[512,768]{1,0:T(8,128)(2,1)}, u32[]{:S(2)}) copy-start(bf16[512,768]{1,0:T(8,128)(2,1)} %get-tuple-element.60.attn_ref) | copy-start | bytes 2359300
  71.6 18.4 %copy-start.3 = (s32[12]{0:T(128)S(1)}, s32[12]{0:T(128)}, u32[]{:S(2)}) copy-start(s32[12]{0:T(128)} %concatenate.3.place_ref) | copy-start | bytes 148
  76.7 6.8 %collective-permute-start.14 = (bf16[48,1536]{1,0:T(8,128)(2,1)S(1)}, bf16[48,1536]{1,0:T(8,128)(2,1)S(1)}, u32[]{:S(2)}, u32[]{:S(2)}) collective-permute-start(bf16[48,1536]{1,0:T(8,128)(2,1)S(1)} %add_convert_fusion.2), channel_id=1, source_target_pairs={{0,128},{1,129},{2,130},{3,131},{4,132},{5,133},{6,134},{7,135},{8... | collective-permute-start | bytes 442376 | tf_op jit(solution)/shard_map/ppermute | solution.py:340
  78.9 6.1 %collective-permute-start.13 = (bf16[48,1536]{1,0:T(8,128)(2,1)S(1)}, bf16[48,1536]{1,0:T(8,128)(2,1)S(1)}, u32[]{:S(2)}, u32[]{:S(2)}) collective-permute-start(bf16[48,1536]{1,0:T(8,128)(2,1)S(1)} %add_convert_fusion.2), channel_id=1, source_target_pairs={{0,129},{1,128},{2,131},{3,130},{4,133},{5,132},{6,135},{7,134},{8... | collective-permute-start | bytes 442376 | tf_op jit(solution)/shard_map/ppermute | solution.py:340
  79.0 6.1 %collective-permute-start.12 = (bf16[48,1536]{1,0:T(8,128)(2,1)S(1)}, bf16[48,1536]{1,0:T(8,128)(2,1)S(1)}, u32[]{:S(2)}, u32[]{:S(2)}) collective-permute-start(bf16[48,1536]{1,0:T(8,128)(2,1)S(1)} %add_convert_fusion.2), channel_id=1, source_target_pairs={{0,1},{1,0},{2,3},{3,2},{4,5},{5,4},{6,7},{7,6},{8,9},{9,8},{10,11... | collective-permute-start | bytes 442376 | tf_op jit(solution)/shard_map/ppermute | solution.py:340
  81.5 8.6 %collective-permute-start.15 = (bf16[512,768]{1,0:T(8,128)(2,1)}, bf16[512,768]{1,0:T(8,128)(2,1)}, u32[]{:S(2)}, u32[]{:S(2)}) collective-permute-start(bf16[512,768]{1,0:T(8,128)(2,1)} %shard_map.97), channel_id=1, source_target_pairs={{0,64},{64,0},{1,65},{65,1},{2,66},{66,2},{3,67},{67,3},{4,68},{68... | collective-permute-start | bytes 2359304 | tf_op jit(solution)/shard_map/ppermute | solution.py:230
  85.2 11.1 %collective-permute-start.16 = (bf16[48,1536]{1,0:T(8,128)(2,1)S(1)}, bf16[48,1536]{1,0:T(8,128)(2,1)S(1)}, u32[]{:S(2)}, u32[]{:S(2)}) collective-permute-start(bf16[48,1536]{1,0:T(8,128)(2,1)S(1)} %add_convert_fusion.1), channel_id=1, source_target_pairs={{0,32},{1,33},{2,34},{3,35},{4,36},{5,37},{6,38},{7,39},{8,40},{9,... | collective-permute-start | bytes 442376 | tf_op jit(solution)/shard_map/ppermute | solution.py:340
  90.1 1.0 copy-start.2
  96.3 7.3 %collective-permute-start.20 = (bf16[48,1536]{1,0:T(8,128)(2,1)S(1)}, bf16[48,1536]{1,0:T(8,128)(2,1)S(1)}, u32[]{:S(2)}, u32[]{:S(2)}) collective-permute-start(bf16[48,1536]{1,0:T(8,128)(2,1)S(1)} %add_convert_fusion), channel_id=1, source_target_pairs={{0,16},{1,17},{2,18},{3,19},{4,20},{5,21},{6,22},{7,23},{8,56},{9,... | collective-permute-start | bytes 442376 | tf_op jit(solution)/shard_map/ppermute | solution.py:340
  97.6 7.2 %collective-permute-start.19 = (bf16[48,1536]{1,0:T(8,128)(2,1)S(1)}, bf16[48,1536]{1,0:T(8,128)(2,1)S(1)}, u32[]{:S(2)}, u32[]{:S(2)}) collective-permute-start(bf16[48,1536]{1,0:T(8,128)(2,1)S(1)} %add_convert_fusion), channel_id=1, source_target_pairs={{0,8},{1,9},{2,10},{3,11},{4,12},{5,13},{6,14},{7,15},{8,0},{9,1},... | collective-permute-start | bytes 442376 | tf_op jit(solution)/shard_map/ppermute | solution.py:340
  99.2 7.7 %collective-permute-start.18 = (bf16[48,1536]{1,0:T(8,128)(2,1)S(1)}, bf16[48,1536]{1,0:T(8,128)(2,1)S(1)}, u32[]{:S(2)}, u32[]{:S(2)}) collective-permute-start(bf16[48,1536]{1,0:T(8,128)(2,1)S(1)} %add_convert_fusion), channel_id=1, source_target_pairs={{0,56},{1,57},{2,58},{3,59},{4,60},{5,61},{6,62},{7,63},{8,16},{9,... | collective-permute-start | bytes 442376 | tf_op jit(solution)/shard_map/ppermute | solution.py:340
  101.1 21.3 %collective-permute-start.17 = (bf16[512,768]{1,0:T(8,128)(2,1)S(1)}, bf16[512,768]{1,0:T(8,128)(2,1)S(1)}, u32[]{:S(2)}, u32[]{:S(2)}) collective-permute-start(bf16[512,768]{1,0:T(8,128)(2,1)S(1)} %get-tuple-element.67), channel_id=1, source_target_pairs={{0,128},{128,0},{1,129},{129,1},{2,130},{130,2},{3,131},{131,3},{4... | collective-permute-start | bytes 2359304 | tf_op jit(solution)/shard_map/ppermute | solution.py:230
  107.0 10.0 %collective-permute-start.23 = (bf16[4,48,1536]{2,1,0:T(8,128)(2,1)S(1)}, bf16[4,48,1536]{2,1,0:T(8,128)(2,1)S(1)}, u32[]{:S(2)}, u32[]{:S(2)}) collective-permute-start(bf16[4,48,1536]{2,1,0:T(8,128)(2,1)S(1)} %pad_maximum_fusion.refs_0_), channel_id=1, source_target_pairs={{0,2},{1,3},{2,0},{3,1},{4,6},{5,7},{6,4},{7,5},{8,10},{9,11},{10,... | collective-permute-start | bytes 1769480 | tf_op jit(solution)/shard_map/ppermute | solution.py:340
  107.3 11.1 %collective-permute-start.21 = (bf16[4,48,1536]{2,1,0:T(8,128)(2,1)S(1)}, bf16[4,48,1536]{2,1,0:T(8,128)(2,1)S(1)}, u32[]{:S(2)}, u32[]{:S(2)}) collective-permute-start(bf16[4,48,1536]{2,1,0:T(8,128)(2,1)S(1)} %pad_maximum_fusion.refs_0_), channel_id=1, source_target_pairs={{0,6},{1,7},{2,4},{3,5},{4,2},{5,3},{6,0},{7,1},{8,14},{9,15},{10,... | collective-permute-start | bytes 1769480 | tf_op jit(solution)/shard_map/ppermute | solution.py:340
  117.0 8.0 %collective-permute-start.24 = (bf16[2,48,1536]{2,1,0:T(8,128)(2,1)S(1)}, bf16[2,48,1536]{2,1,0:T(8,128)(2,1)S(1)}, u32[]{:S(2)}, u32[]{:S(2)}) collective-permute-start(bf16[2,48,1536]{2,1,0:T(8,128)(2,1)S(1)} %slice.20), channel_id=1, source_target_pairs={{0,6},{1,7},{2,4},{3,5},{4,2},{5,3},{6,0},{7,1},{8,14},{9,15},{10,... | collective-permute-start | bytes 884744 | tf_op jit(solution)/shard_map/ppermute | solution.py:340
  118.5 6.8 %collective-permute-start.22 = (bf16[2,48,1536]{2,1,0:T(8,128)(2,1)S(1)}, bf16[2,48,1536]{2,1,0:T(8,128)(2,1)S(1)}, u32[]{:S(2)}, u32[]{:S(2)}) collective-permute-start(bf16[2,48,1536]{2,1,0:T(8,128)(2,1)S(1)} %slice.18), channel_id=1, source_target_pairs={{0,2},{1,3},{2,0},{3,1},{4,6},{5,7},{6,4},{7,5},{8,10},{9,11},{10,... | collective-permute-start | bytes 884744 | tf_op jit(solution)/shard_map/ppermute | solution.py:340
where the time goes:
time: 128 us; the launch traced here: 127 us
  Pallas kernels  56.7 us (44%)
  starting transfers between devices  41 us (32%)
  waiting for transfers between devices  22.4 us (18%)
  local copies, waits for them, and re-layouts  4.14 us (3%)
  other arithmetic  1.72 us (1%)
    pallas_call x9, Pallas kernels, call(): pl.pallas_call(kernel, grid_spec=pltpu.PrefetchScalarGridSpec(num_scalar_...  56.7 us
    ppermute x20, starting transfers between devices, move(): return lax.ppermute(value, AXES, table)  34.1 us
    ppermute x20, waiting for transfers between devices, move(): return lax.ppermute(value, AXES, table)  22.2 us
    ppermute x5, starting transfers between devices, swap(): return lax.ppermute(value, axis, [(0, 1), (1, 0)])  6.92 us
  transfers between devices with their start and end apart: 25, of which 15 were waited for; matrix products, arithmetic and copies ran while one was open for 3% of the time, Pallas kernels for 38%

commit v1 on v0

--- a/solution.py
+++ b/solution.py
@@ -195,14 +195,19 @@
     out_ref[...] = jnp.dot(attn_ref[...], w_ref[...], preferred_element_type=F32).astype(BF)
 
 
-def mixed_kernel(place_ref, attn_ref, w_ref, recv_ref, pick_ref, mixed_ref, send_ref, keep_ref):
+def mixed_kernel(place_ref, attn_ref, w_ref, recv_ref, pick_ref, mixed_ref, send_ref, keep_ref, hot_ref):
     rows = attn_ref.shape[0]
+
+    @pl.when(pl.program_id(0) == 0)
+    def _():
+        row = lax.broadcasted_iota(jnp.int32, (rows, rows), 0)
+        for half in range(2):
+            hot_ref[half] = jnp.where(pick_ref[half : half + 1, :] == row, 1.0, 0.0).astype(BF).T
+
     mixed = (jnp.dot(attn_ref[...], w_ref[...], preferred_element_type=F32) + recv_ref[...].astype(F32)).astype(BF)
     mixed_ref[...] = mixed
-    row = lax.broadcasted_iota(jnp.int32, (rows, rows), 1)
     for half, out in ((0, send_ref), (1, keep_ref)):
-        hot = jnp.where(pick_ref[half * rows : half * rows + rows, :] == row, 1.0, 0.0).astype(BF)
-        out[...] = jnp.dot(hot, mixed, preferred_element_type=F32).astype(BF)
+        out[...] = jnp.dot(hot_ref[half], mixed, preferred_element_type=F32).astype(BF)
 
 
 def call(kernel, place, grid, in_specs, out_specs, out_shape, scratch, flops, nbytes, args, alias=None, limit=VMEM_LIMIT):
@@ -357,9 +362,9 @@
     width = rights[0].shape[1]
     piece = part // 4
     return call(
-        grad_kernel, place, (width // GROUP,),
-        [whole(lefts[0].shape)] * 4 + [columns(rows, GROUP)] * 4, [columns(piece, GROUP)] * 4,
-        [jax.ShapeDtypeStruct((piece, width), BF)] * 4, [pltpu.VMEM((part, GROUP), F32)],
+        grad_kernel, place, (width // (2 * GROUP),),
+        [whole(lefts[0].shape)] * 4 + [columns(rows, 2 * GROUP)] * 4, [columns(piece, 2 * GROUP)] * 4,
+        [jax.ShapeDtypeStruct((piece, width), BF)] * 4, [pltpu.VMEM((part, 2 * GROUP), F32)],
         12 * 10**8, 8 * 10**6, (*lefts, *rights), limit=BIG_VMEM,
     )
 
@@ -415,7 +420,6 @@
     by_slot = jnp.sum(jnp.where(order[:, :, None], picks[None], 0), axis=1).reshape(2, rows)
     local = by_slot - seq * rows
     local = jnp.stack([jnp.where(seq == 0, local[1], local[0]), jnp.where(seq == 0, local[0], local[1])])
-    local = local.reshape(2 * rows, 1)
 
     lefts = [turned[0]] + [move(t, table) for t, table in zip(turned[1:], first)]
 
@@ -438,8 +442,8 @@
     mixed, send, keep = call(
         mixed_kernel, place, (groups,),
         [whole((rows, share)), pl.BlockSpec((share, GROUP), lambda g, s: (0, s[1] * groups + g)),
-         columns(rows, GROUP), whole((2 * rows, 1))],
-        [columns(rows, GROUP)] * 3, [shape] * 3, [], 14 * 10**8, 6 * 10**6, (attn, out_weight, recv, local),
+         columns(rows, GROUP), whole((2, rows))],
+        [columns(rows, GROUP)] * 3, [shape] * 3, [pltpu.VMEM((2, rows, rows), BF)], 14 * 10**8, 6 * 10**6, (attn, out_weight, recv, local),
     )
     over_z, send = lax.optimization_barrier((over_z, send))
     grad = add(grad, over_z)

time: 128 us -> 127 us (level)
  local copies, waits for them, and re-layouts: 4.14 us -> 2 us
  starting transfers between devices: 41 us -> 42.7 us
  Pallas kernels: 56.7 us -> 55.2 us
    pallas_call x9, Pallas kernels: 56.7 us -> 55.2 us  [call(): pl.pallas_call(kernel, grid_spec=pltpu.PrefetchScalarGridSpec(num_scalar_...]
  transfers between devices with their start and end apart: 25 -> 25, of which waited for: 15 -> 15; matrix products, arithmetic and copies ran while one was open for 3% -> 2% of each run, Pallas kernels for 38% -> 38%
where the time goes in v1:
time: 127 us; the launch traced here: 126 us
  Pallas kernels  55.2 us (43%)
  starting transfers between devices  42.7 us (34%)
  waiting for transfers between devices  23.5 us (19%)
  local copies, waits for them, and re-layouts  2 us (2%)
  other arithmetic  1.76 us (1%)
    pallas_call x9, Pallas kernels, call(): pl.pallas_call(kernel, grid_spec=pltpu.PrefetchScalarGridSpec(num_scalar_...  55.2 us
    ppermute x20, starting transfers between devices, move(): return lax.ppermute(value, AXES, table)  34.9 us
    ppermute x20, waiting for transfers between devices, move(): return lax.ppermute(value, AXES, table)  23.2 us
    ppermute x5, starting transfers between devices, swap(): return lax.ppermute(value, axis, [(0, 1), (1, 0)])  7.87 us
  transfers between devices with their start and end apart: 25, of which 15 were waited for; matrix products, arithmetic and copies ran while one was open for 2% of the time, Pallas kernels for 38%

profile of v1, /device:TPU:2, one launch (start us, length us, event | category | flops | bytes accessed | tf_op | source)
XLA Modules:
  0.0 125.9 jit_solution(18018963804691160510)
XLA Ops:
  0.6 1.7 %collective-permute-start.3 = (bf16[512,1536]{1,0:T(8,128)(2,1)}, bf16[512,1536]{1,0:T(8,128)(2,1)S(1)}, u32[]{:S(2)}, u32[]{:S(2)}) collective-permute-start(bf16[512,1536]{1,0:T(8,128)(2,1)} %bitcast.22), channel_id=1, source_target_pairs={{0,2},{1,3},{2,0},{3,1},{4,6},{5,7},{6,4},{7,5},{8,10},{9,11},{10,... | collective-permute-start | bytes 4718600 | tf_op jit(solution)/shard_map/ppermute | solution.py:345
  2.3 2.2 %collective-permute-start.2 = (bf16[512,1536]{1,0:T(8,128)(2,1)}, bf16[512,1536]{1,0:T(8,128)(2,1)}, u32[]{:S(2)}, u32[]{:S(2)}) collective-permute-start(bf16[512,1536]{1,0:T(8,128)(2,1)} %bitcast.23), channel_id=1, source_target_pairs={{0,6},{1,7},{2,4},{3,5},{4,2},{5,3},{6,0},{7,1},{8,14},{9,15},{10,... | collective-permute-start | bytes 4718600 | tf_op jit(solution)/shard_map/ppermute | solution.py:345
  4.5 2.4 %collective-permute-start.1 = (bf16[512,768]{1,0:T(8,128)(2,1)}, bf16[512,768]{1,0:T(8,128)(2,1)}, u32[]{:S(2)}, u32[]{:S(2)}) collective-permute-start(bf16[512,768]{1,0:T(8,128)(2,1)} %bitcast.26), channel_id=1, source_target_pairs={{0,64},{64,0},{1,65},{65,1},{2,66},{66,2},{3,67},{67,3},{4,68},{68... | collective-permute-start | bytes 2359304 | tf_op jit(solution)/shard_map/ppermute | solution.py:235
  6.9 2.1 %collective-permute-start = (bf16[512,768]{1,0:T(8,128)(2,1)}, bf16[512,768]{1,0:T(8,128)(2,1)}, u32[]{:S(2)}, u32[]{:S(2)}) collective-permute-start(bf16[512,768]{1,0:T(8,128)(2,1)} %bitcast.27), channel_id=1, source_target_pairs={{0,128},{128,0},{1,129},{129,1},{2,130},{130,2},{3,131},{131,3},{4... | collective-permute-start | bytes 2359304 | tf_op jit(solution)/shard_map/ppermute | solution.py:235
  9.0 1.2 concatenate.3.place_ref
  10.2 17.6 %shard_map.94 = (bf16[3,512,256]{2,1,0:T(8,128)(2,1)}, bf16[3,512,512]{2,1,0:T(8,128)(2,1)}) custom-call(s32[12]{0:T(128)} %concatenate.3.place_ref, bf16[512,768]{1,0:T(8,128)(2,1)} %bitcast.28, bf16[512,768]{1,0:T(8,128)(2,1)} %collective-permute-done.1.oth_ref, bf16[3,1536,768]{2,1,0:T(8,128)(2,1)} %w_ref.5), custom_call_target="tpu_custom_call" | custom-call | flops 100000000 | bytes 1000000 | tf_op jit(solution)/shard_map/pallas_call | solution.py:214
  27.9 0.3 collective-permute-done.own_ref
  28.2 3.5 %collective-permute-start.8 = (bf16[512,1536]{1,0:T(8,128)(2,1)S(1)}, bf16[512,1536]{1,0:T(8,128)(2,1)}, u32[]{:S(2)}, u32[]{:S(2)}) collective-permute-start(bf16[512,1536]{1,0:T(8,128)(2,1)S(1)} %bitcast.25), channel_id=1, source_target_pairs={{0,4},{1,5},{2,6},{3,7},{4,0},{5,1},{6,2},{7,3},{8,12},{9,13},{10,... | collective-permute-start | bytes 4718600 | tf_op jit(solution)/shard_map/ppermute | solution.py:345
  31.7 15.4 %shard_map.95 = (bf16[512,768]{1,0:T(8,128)(2,1)}, bf16[192,512]{1,0:T(8,128)(2,1)}, bf16[192,512]{1,0:T(8,128)(2,1)}, bf16[192,512]{1,0:T(8,128)(2,1)}, bf16[192,512]{1,0:T(8,128)(2,1)}) custom-call(s32[12]{0:T(128)} %concatenate.3.place_ref, bf16[512,768]{1,0:T(8,128)(2,1)} %collective-permute-done.own_ref, ...), custom_call_target="tpu_custom_call" | custom-call | flops 1000000000 | bytes 1000000 | tf_op jit(solution)/shard_map/pallas_call | solution.py:214
  47.2 0.2 reduce-window.9
  47.3 2.2 %collective-permute-start.5 = (bf16[192,512]{1,0:T(8,128)(2,1)}, bf16[192,512]{1,0:T(8,128)(2,1)S(1)}, u32[]{:S(2)}, u32[]{:S(2)}) collective-permute-start(bf16[192,512]{1,0:T(8,128)(2,1)} %get-tuple-element.42), channel_id=1, source_target_pairs={{0,6},{1,7},{2,4},{3,5},{4,2},{5,3},{6,0},{7,1},{8,14},{9,15},{10,... | collective-permute-start | bytes 589832 | tf_op jit(solution)/shard_map/ppermute | solution.py:345
  49.5 0.1 collective-permute-start.6
  49.7 2.4 %collective-permute-start.7 = (bf16[192,512]{1,0:T(8,128)(2,1)}, bf16[192,512]{1,0:T(8,128)(2,1)S(1)}, u32[]{:S(2)}, u32[]{:S(2)}) collective-permute-start(bf16[192,512]{1,0:T(8,128)(2,1)} %get-tuple-element.44), channel_id=1, source_target_pairs={{0,4},{1,5},{2,6},{3,7},{4,0},{5,1},{6,2},{7,3},{8,12},{9,13},{10,... | collective-permute-start | bytes 589832 | tf_op jit(solution)/shard_map/ppermute | solution.py:345
  52.1 0.2 fusion.1
  52.4 2.0 %collective-permute-done.5.refs_1_ = bf16[192,512]{1,0:T(8,128)(2,1)S(1)} collective-permute-done((bf16[192,512]{1,0:T(8,128)(2,1)}, bf16[192,512]{1,0:T(8,128)(2,1)S(1)}, u32[]{:S(2)}, u32[]{:S(2)}) %collective-permute-start.5) | collective-permute-done | bytes 196640 | tf_op jit(solution)/shard_map/ppermute | solution.py:345
  54.4 1.0 collective-permute-done.6.refs_2_
  55.4 2.6 %collective-permute-done.7.refs_3_ = bf16[192,512]{1,0:T(8,128)(2,1)S(1)} collective-permute-done((bf16[192,512]{1,0:T(8,128)(2,1)}, bf16[192,512]{1,0:T(8,128)(2,1)S(1)}, u32[]{:S(2)}, u32[]{:S(2)}) %collective-permute-start.7) | collective-permute-done | bytes 196640 | tf_op jit(solution)/shard_map/ppermute | solution.py:345
  58.0 0.7 copy-done.7
  58.7 6.2 %shard_map.96 = (bf16[48,1536]{1,0:T(8,128)(2,1)}, bf16[48,1536]{1,0:T(8,128)(2,1)}, bf16[48,1536]{1,0:T(8,128)(2,1)}, bf16[48,1536]{1,0:T(8,128)(2,1)}) custom-call(s32[12]{0:T(128)} %concatenate.3.place_ref, bf16[192,512]{1,0:T(8,128)(2,1)} %get-tuple-element.41.refs_0_, bf16[192,512]{1,0:T(8,128)(2,1)} %copy-done.5, bf16[192,512]{1,0:T(8,128)(2,1)} %copy-done.6, ...), custom_call_target="tpu_custom_call" | custom-call | flops 1200000000 | bytes 8000000 | tf_op jit(solution)/shard_map/pallas_call | solution.py:214
  64.9 3.2 %collective-permute-start.9 = (bf16[48,1536]{1,0:T(8,128)(2,1)}, bf16[48,1536]{1,0:T(8,128)(2,1)S(1)}, u32[]{:S(2)}, u32[]{:S(2)}) collective-permute-start(bf16[48,1536]{1,0:T(8,128)(2,1)} %get-tuple-element.51), channel_id=1, source_target_pairs={{0,56},{1,57},{2,58},{3,59},{4,60},{5,61},{6,62},{7,63},{8,16},{9,... | collective-permute-start | bytes 442376 | tf_op jit(solution)/shard_map/ppermute | solution.py:345
  68.1 2.5 %collective-permute-start.11 = (bf16[48,1536]{1,0:T(8,128)(2,1)}, bf16[48,1536]{1,0:T(8,128)(2,1)S(1)}, u32[]{:S(2)}, u32[]{:S(2)}) collective-permute-start(bf16[48,1536]{1,0:T(8,128)(2,1)} %get-tuple-element.53), channel_id=1, source_target_pairs={{0,16},{1,17},{2,18},{3,19},{4,20},{5,21},{6,22},{7,23},{8,56},{9,... | collective-permute-start | bytes 442376 | tf_op jit(solution)/shard_map/ppermute | solution.py:345
  70.6 4.8 %shard_map.97 = bf16[512,768]{1,0:T(8,128)(2,1)} custom-call(s32[12]{0:T(128)} %concatenate.3.place_ref, bf16[512,768]{1,0:T(8,128)(2,1)} %get-tuple-element.60.attn_ref, bf16[768,1536]{1,0:T(8,128)(2,1)} %w_ref.7), custom_call_target="tpu_custom_call" | custom-call | flops 600000000 | bytes 3000000 | tf_op jit(solution)/shard_map/pallas_call | solution.py:214
  75.3 0.2 collective-permute-done.11
  75.7 2.2 %collective-permute-start.14 = (bf16[48,1536]{1,0:T(8,128)(2,1)S(1)}, bf16[48,1536]{1,0:T(8,128)(2,1)S(1)}, u32[]{:S(2)}, u32[]{:S(2)}) collective-permute-start(bf16[48,1536]{1,0:T(8,128)(2,1)S(1)} %add_convert_fusion.2), channel_id=1, source_target_pairs={{0,128},{1,129},{2,130},{3,131},{4,132},{5,133},{6,134},{7,135},{8... | collective-permute-start | bytes 442376 | tf_op jit(solution)/shard_map/ppermute | solution.py:345
  77.9 2.5 %collective-permute-start.12 = (bf16[48,1536]{1,0:T(8,128)(2,1)S(1)}, bf16[48,1536]{1,0:T(8,128)(2,1)S(1)}, u32[]{:S(2)}, u32[]{:S(2)}) collective-permute-start(bf16[48,1536]{1,0:T(8,128)(2,1)S(1)} %add_convert_fusion.2), channel_id=1, source_target_pairs={{0,1},{1,0},{2,3},{3,2},{4,5},{5,4},{6,7},{7,6},{8,9},{9,8},{10,11... | collective-permute-start | bytes 442376 | tf_op jit(solution)/shard_map/ppermute | solution.py:345
  80.5 2.0 %collective-permute-done.14 = bf16[48,1536]{1,0:T(8,128)(2,1)S(1)} collective-permute-done((bf16[48,1536]{1,0:T(8,128)(2,1)S(1)}, bf16[48,1536]{1,0:T(8,128)(2,1)S(1)}, u32[]{:S(2)}, u32[]{:S(2)}) %collective-permute-start.14) | collective-permute-done | bytes 147488 | tf_op jit(solution)/shard_map/ppermute | solution.py:345
  82.5 1.5 %collective-permute-done.13 = bf16[48,1536]{1,0:T(8,128)(2,1)S(1)} collective-permute-done((bf16[48,1536]{1,0:T(8,128)(2,1)S(1)}, bf16[48,1536]{1,0:T(8,128)(2,1)S(1)}, u32[]{:S(2)}, u32[]{:S(2)}) %collective-permute-start.13) | collective-permute-done | bytes 147488 | tf_op jit(solution)/shard_map/ppermute | solution.py:345
  84.1 3.8 %collective-permute-start.16 = (bf16[48,1536]{1,0:T(8,128)(2,1)S(1)}, bf16[48,1536]{1,0:T(8,128)(2,1)S(1)}, u32[]{:S(2)}, u32[]{:S(2)}) collective-permute-start(bf16[48,1536]{1,0:T(8,128)(2,1)S(1)} %add_convert_fusion.1), channel_id=1, source_target_pairs={{0,32},{1,33},{2,34},{3,35},{4,36},{5,37},{6,38},{7,39},{8,40},{9,... | collective-permute-start | bytes 442376 | tf_op jit(solution)/shard_map/ppermute | solution.py:345
  88.0 4.6 %shard_map.98 = (bf16[512,768]{1,0:T(8,128)(2,1)}, bf16[512,768]{1,0:T(8,128)(2,1)S(1)}, bf16[512,768]{1,0:T(8,128)(2,1)S(1)}) custom-call(s32[12]{0:T(128)S(1)} %copy-done.2, bf16[512,768]{1,0:T(8,128)(2,1)S(1)} %copy-done.1, bf16[768,1536]{1,0:T(8,128)(2,1)S(1)} %copy-done, bf16[512,768]{1,0:T(8,128)(2,1)S(1)} %collective-permute-done.15.recv_ref, ...), custom_call_target="tpu_custom_call" | custom-call | flops 1400000000 | bytes 6000000 | tf_op jit(solution)/shard_map/pallas_call | solution.py:214
  92.6 0.8 collective-permute-done.16
  93.5 3.0 %collective-permute-start.20 = (bf16[48,1536]{1,0:T(8,128)(2,1)S(1)}, bf16[48,1536]{1,0:T(8,128)(2,1)S(1)}, u32[]{:S(2)}, u32[]{:S(2)}) collective-permute-start(bf16[48,1536]{1,0:T(8,128)(2,1)S(1)} %add_convert_fusion), channel_id=1, source_target_pairs={{0,16},{1,17},{2,18},{3,19},{4,20},{5,21},{6,22},{7,23},{8,56},{9,... | collective-permute-start | bytes 442376 | tf_op jit(solution)/shard_map/ppermute | solution.py:345
  96.5 1.7 %collective-permute-start.19 = (bf16[48,1536]{1,0:T(8,128)(2,1)S(1)}, bf16[48,1536]{1,0:T(8,128)(2,1)S(1)}, u32[]{:S(2)}, u32[]{:S(2)}) collective-permute-start(bf16[48,1536]{1,0:T(8,128)(2,1)S(1)} %add_convert_fusion), channel_id=1, source_target_pairs={{0,8},{1,9},{2,10},{3,11},{4,12},{5,13},{6,14},{7,15},{8,0},{9,1},... | collective-permute-start | bytes 442376 | tf_op jit(solution)/shard_map/ppermute | solution.py:345
  98.2 0.1 collective-permute-start.18
  98.3 3.3 %collective-permute-start.17 = (bf16[512,768]{1,0:T(8,128)(2,1)S(1)}, bf16[512,768]{1,0:T(8,128)(2,1)S(1)}, u32[]{:S(2)}, u32[]{:S(2)}) collective-permute-start(bf16[512,768]{1,0:T(8,128)(2,1)S(1)} %get-tuple-element.67), channel_id=1, source_target_pairs={{0,128},{128,0},{1,129},{129,1},{2,130},{130,2},{3,131},{131,3},{4... | collective-permute-start | bytes 2359304 | tf_op jit(solution)/shard_map/ppermute | solution.py:235
  101.6 3.5 %collective-permute-done.19 = bf16[48,1536]{1,0:T(8,128)(2,1)S(1)} collective-permute-done((bf16[48,1536]{1,0:T(8,128)(2,1)S(1)}, bf16[48,1536]{1,0:T(8,128)(2,1)S(1)}, u32[]{:S(2)}, u32[]{:S(2)}) %collective-permute-start.19) | collective-permute-done | bytes 147488 | tf_op jit(solution)/shard_map/ppermute | solution.py:345
  105.1 1.0 collective-permute-done.18
  106.2 0.1 collective-permute-start.23
  106.3 1.9 %collective-permute-start.21 = (bf16[4,48,1536]{2,1,0:T(8,128)(2,1)S(1)}, bf16[4,48,1536]{2,1,0:T(8,128)(2,1)S(1)}, u32[]{:S(2)}, u32[]{:S(2)}) collective-permute-start(bf16[4,48,1536]{2,1,0:T(8,128)(2,1)S(1)} %pad_maximum_fusion.refs_0_), channel_id=1, source_target_pairs={{0,6},{1,7},{2,4},{3,5},{4,2},{5,3},{6,0},{7,1},{8,14},{9,15},{10,... | collective-permute-start | bytes 1769480 | tf_op jit(solution)/shard_map/ppermute | solution.py:345
  108.2 1.6 %shard_map.99.refs_1_ = f32[768,1536]{1,0:T(8,128)} custom-call(s32[12]{0:T(128)S(1)} %copy-done.2, bf16[4,48,1536]{2,1,0:T(8,128)(2,1)S(1)} %pad_maximum_fusion.refs_0_), custom_call_target="tpu_custom_call" | custom-call | flops 1000000 | bytes 2000000 | tf_op jit(solution)/shard_map/pallas_call | solution.py:214
  109.8 6.4 %collective-permute-done.23.refs_0_ = bf16[4,48,1536]{2,1,0:T(8,128)(2,1)S(1)} collective-permute-done((bf16[4,48,1536]{2,1,0:T(8,128)(2,1)S(1)}, bf16[4,48,1536]{2,1,0:T(8,128)(2,1)S(1)}, u32[]{:S(2)}, u32[]{:S(2)}) %collective-permute-start.23) | collective-permute-done | bytes 589856 | tf_op jit(solution)/shard_map/ppermute | solution.py:345
  116.2 1.0 collective-permute-start.24
  117.2 0.3 collective-permute-done.21.refs_0_
  117.5 0.8 collective-permute-start.22
  118.3 1.6 %shard_map.100.refs_1_ = f32[768,1536]{1,0:T(8,128)} custom-call(s32[12]{0:T(128)S(1)} %copy-done.2, bf16[4,48,1536]{2,1,0:T(8,128)(2,1)S(1)} %collective-permute-done.21.refs_0_, f32[768,1536]{1,0:T(8,128)} %shard_map.99.refs_1_), custom_call_target="tpu_custom_call", output_to_operand_aliasing={{}: (2, {})} | custom-call | flops 1000000 | bytes 2000000 | tf_op jit(solution)/shard_map/pallas_call | solution.py:214
  119.9 1.6 %shard_map.101.refs_2_ = f32[768,1536]{1,0:T(8,128)} custom-call(s32[12]{0:T(128)S(1)} %copy-done.2, bf16[4,48,1536]{2,1,0:T(8,128)(2,1)S(1)} %collective-permute-done.23.refs_0_, f32[768,1536]{1,0:T(8,128)} %shard_map.100.refs_1_), custom_call_target="tpu_custom_call", output_to_operand_aliasing={{}: (2, {})} | custom-call | flops 1000000 | bytes 2000000 | tf_op jit(solution)/shard_map/pallas_call | solution.py:214
  121.6 1.0 add_bitcast_fusion
  122.6 1.6 %collective-permute-done.24.refs_1_ = bf16[2,48,1536]{2,1,0:T(8,128)(2,1)S(1)} collective-permute-done((bf16[2,48,1536]{2,1,0:T(8,128)(2,1)S(1)}, bf16[2,48,1536]{2,1,0:T(8,128)(2,1)S(1)}, u32[]{:S(2)}, u32[]{:S(2)}) %collective-permute-start.24) | collective-permute-done | bytes 294944 | tf_op jit(solution)/shard_map/ppermute | solution.py:345
  124.3 1.6 %shard_map.102 = f32[768,1536]{1,0:T(8,128)} custom-call(s32[12]{0:T(128)S(1)} %copy-done.2, bf16[2,48,1536]{2,1,0:T(8,128)(2,1)S(1)} %collective-permute-done.22.refs_0_, bf16[2,48,1536]{2,1,0:T(8,128)(2,1)S(1)} %collective-permute-done.24.refs_1_, f32[768,1536]{1,0:T(8,128)} %shard_map.101.refs_2_), custom_call_target="tpu_custom_call", output_to_operand_aliasing={{}: (3, {})} | custom-call | flops 1000000 | bytes 2000000 | tf_op jit(solution)/shard_map/pallas_call | solution.py:214
  (52 shorter events, 0.8 us)
Async XLA Ops:
  0.6 27.5 %collective-permute-start.3 = (bf16[512,1536]{1,0:T(8,128)(2,1)}, bf16[512,1536]{1,0:T(8,128)(2,1)S(1)}, u32[]{:S(2)}, u32[]{:S(2)}) collective-permute-start(bf16[512,1536]{1,0:T(8,128)(2,1)} %bitcast.22), channel_id=1, source_target_pairs={{0,2},{1,3},{2,0},{3,1},{4,6},{5,7},{6,4},{7,5},{8,10},{9,11},{10,... | collective-permute-start | bytes 4718600 | tf_op jit(solution)/shard_map/ppermute | solution.py:345
  2.3 25.8 %collective-permute-start.2 = (bf16[512,1536]{1,0:T(8,128)(2,1)}, bf16[512,1536]{1,0:T(8,128)(2,1)}, u32[]{:S(2)}, u32[]{:S(2)}) collective-permute-start(bf16[512,1536]{1,0:T(8,128)(2,1)} %bitcast.23), channel_id=1, source_target_pairs={{0,6},{1,7},{2,4},{3,5},{4,2},{5,3},{6,0},{7,1},{8,14},{9,15},{10,... | collective-permute-start | bytes 4718600 | tf_op jit(solution)/shard_map/ppermute | solution.py:345
  4.5 5.8 %collective-permute-start.1 = (bf16[512,768]{1,0:T(8,128)(2,1)}, bf16[512,768]{1,0:T(8,128)(2,1)}, u32[]{:S(2)}, u32[]{:S(2)}) collective-permute-start(bf16[512,768]{1,0:T(8,128)(2,1)} %bitcast.26), channel_id=1, source_target_pairs={{0,64},{64,0},{1,65},{65,1},{2,66},{66,2},{3,67},{67,3},{4,68},{68... | collective-permute-start | bytes 2359304 | tf_op jit(solution)/shard_map/ppermute | solution.py:235
  6.9 21.3 %collective-permute-start = (bf16[512,768]{1,0:T(8,128)(2,1)}, bf16[512,768]{1,0:T(8,128)(2,1)}, u32[]{:S(2)}, u32[]{:S(2)}) collective-permute-start(bf16[512,768]{1,0:T(8,128)(2,1)} %bitcast.27), channel_id=1, source_target_pairs={{0,128},{128,0},{1,129},{129,1},{2,130},{130,2},{3,131},{131,3},{4... | collective-permute-start | bytes 2359304 | tf_op jit(solution)/shard_map/ppermute | solution.py:235
  10.2 18.0 %copy-start.3 = (bf16[1,512,1536]{2,1,0:T(8,128)(2,1)S(1)}, bf16[1,512,1536]{2,1,0:T(8,128)(2,1)}, u32[]{:S(2)}) copy-start(bf16[1,512,1536]{2,1,0:T(8,128)(2,1)} %param.11) | copy-start | bytes 4718596
  28.1 19.0 %copy-start.4 = (bf16[512,1536]{1,0:T(8,128)(2,1)}, bf16[512,1536]{1,0:T(8,128)(2,1)S(1)}, u32[]{:S(2)}) copy-start(bf16[512,1536]{1,0:T(8,128)(2,1)S(1)} %collective-permute-done.3.refs_6_) | copy-start | bytes 4718596
  28.1 3.6 %collective-permute-start.4 = (bf16[512,768]{1,0:T(8,128)(2,1)}, bf16[512,768]{1,0:T(8,128)(2,1)}, u32[]{:S(2)}, u32[]{:S(2)}) collective-permute-start(bf16[512,768]{1,0:T(8,128)(2,1)} %collective-permute-done.own_ref), channel_id=1, source_target_pairs={{0,64},{64,0},{1,65},{65,1},{2,66},{66,2},{3,67},{67,3},{4,68},{68... | collective-permute-start | bytes 2359304 | tf_op jit(solution)/shard_map/ppermute | solution.py:235
  28.2 24.1 %collective-permute-start.8 = (bf16[512,1536]{1,0:T(8,128)(2,1)S(1)}, bf16[512,1536]{1,0:T(8,128)(2,1)}, u32[]{:S(2)}, u32[]{:S(2)}) collective-permute-start(bf16[512,1536]{1,0:T(8,128)(2,1)S(1)} %bitcast.25), channel_id=1, source_target_pairs={{0,4},{1,5},{2,6},{3,7},{4,0},{5,1},{6,2},{7,3},{8,12},{9,13},{10,... | collective-permute-start | bytes 4718600 | tf_op jit(solution)/shard_map/ppermute | solution.py:345
  31.7 15.4 %copy-start.10 = (s32[1,8]{1,0:T(1,128)S(1)}, s32[1,8]{1,0:T(1,128)}, u32[]{:S(2)}) copy-start(s32[1,8]{1,0:T(1,128)} %param.8) | copy-start | bytes 100
  31.7 20.4 %copy-start.9 = (s32[1,8,128]{2,1,0:T(8,128)S(1)}, s32[1,8,128]{2,1,0:T(8,128)}, u32[]{:S(2)}) copy-start(s32[1,8,128]{2,1,0:T(8,128)} %param.10) | copy-start | bytes 12292
  31.7 20.6 %copy-start.11 = (s32[1,8]{1,0:T(1,128)S(1)}, s32[1,8]{1,0:T(1,128)}, u32[]{:S(2)}) copy-start(s32[1,8]{1,0:T(1,128)} %param.9) | copy-start | bytes 100
  47.3 7.1 %collective-permute-start.5 = (bf16[192,512]{1,0:T(8,128)(2,1)}, bf16[192,512]{1,0:T(8,128)(2,1)S(1)}, u32[]{:S(2)}, u32[]{:S(2)}) collective-permute-start(bf16[192,512]{1,0:T(8,128)(2,1)} %get-tuple-element.42), channel_id=1, source_target_pairs={{0,6},{1,7},{2,4},{3,5},{4,2},{5,3},{6,0},{7,1},{8,14},{9,15},{10,... | collective-permute-start | bytes 589832 | tf_op jit(solution)/shard_map/ppermute | solution.py:345
  49.5 5.9 %collective-permute-start.6 = (bf16[192,512]{1,0:T(8,128)(2,1)}, bf16[192,512]{1,0:T(8,128)(2,1)S(1)}, u32[]{:S(2)}, u32[]{:S(2)}) collective-permute-start(bf16[192,512]{1,0:T(8,128)(2,1)} %get-tuple-element.43), channel_id=1, source_target_pairs={{0,2},{1,3},{2,0},{3,1},{4,6},{5,7},{6,4},{7,5},{8,10},{9,11},{10,... | collective-permute-start | bytes 589832 | tf_op jit(solution)/shard_map/ppermute | solution.py:345
  49.7 8.4 %collective-permute-start.7 = (bf16[192,512]{1,0:T(8,128)(2,1)}, bf16[192,512]{1,0:T(8,128)(2,1)S(1)}, u32[]{:S(2)}, u32[]{:S(2)}) collective-permute-start(bf16[192,512]{1,0:T(8,128)(2,1)} %get-tuple-element.44), channel_id=1, source_target_pairs={{0,4},{1,5},{2,6},{3,7},{4,0},{5,1},{6,2},{7,3},{8,12},{9,13},{10,... | collective-permute-start | bytes 589832 | tf_op jit(solution)/shard_map/ppermute | solution.py:345
  54.4 3.6 %copy-start.5 = (bf16[192,512]{1,0:T(8,128)(2,1)}, bf16[192,512]{1,0:T(8,128)(2,1)S(1)}, u32[]{:S(2)}) copy-start(bf16[192,512]{1,0:T(8,128)(2,1)S(1)} %collective-permute-done.5.refs_1_) | copy-start | bytes 589828
  55.4 2.6 %copy-start.6 = (bf16[192,512]{1,0:T(8,128)(2,1)}, bf16[192,512]{1,0:T(8,128)(2,1)S(1)}, u32[]{:S(2)}) copy-start(bf16[192,512]{1,0:T(8,128)(2,1)S(1)} %collective-permute-done.6.refs_2_) | copy-start | bytes 589828
  58.0 0.7 copy-start.7
  64.9 10.7 %copy-start.8 = (bf16[48,1536]{1,0:T(8,128)(2,1)S(1)}, bf16[48,1536]{1,0:T(8,128)(2,1)}, u32[]{:S(2)}) copy-start(bf16[48,1536]{1,0:T(8,128)(2,1)} %get-tuple-element.50) | copy-start | bytes 442372
  64.9 10.7 %collective-permute-start.9 = (bf16[48,1536]{1,0:T(8,128)(2,1)}, bf16[48,1536]{1,0:T(8,128)(2,1)S(1)}, u32[]{:S(2)}, u32[]{:S(2)}) collective-permute-start(bf16[48,1536]{1,0:T(8,128)(2,1)} %get-tuple-element.51), channel_id=1, source_target_pairs={{0,56},{1,57},{2,58},{3,59},{4,60},{5,61},{6,62},{7,63},{8,16},{9,... | collective-permute-start | bytes 442376 | tf_op jit(solution)/shard_map/ppermute | solution.py:345
  68.1 7.5 %collective-permute-start.10 = (bf16[48,1536]{1,0:T(8,128)(2,1)}, bf16[48,1536]{1,0:T(8,128)(2,1)S(1)}, u32[]{:S(2)}, u32[]{:S(2)}) collective-permute-start(bf16[48,1536]{1,0:T(8,128)(2,1)} %get-tuple-element.52), channel_id=1, source_target_pairs={{0,8},{1,9},{2,10},{3,11},{4,12},{5,13},{6,14},{7,15},{8,0},{9,1},... | collective-permute-start | bytes 442376 | tf_op jit(solution)/shard_map/ppermute | solution.py:345
  68.1 7.5 %collective-permute-start.11 = (bf16[48,1536]{1,0:T(8,128)(2,1)}, bf16[48,1536]{1,0:T(8,128)(2,1)S(1)}, u32[]{:S(2)}, u32[]{:S(2)}) collective-permute-start(bf16[48,1536]{1,0:T(8,128)(2,1)} %get-tuple-element.53), channel_id=1, source_target_pairs={{0,16},{1,17},{2,18},{3,19},{4,20},{5,21},{6,22},{7,23},{8,56},{9,... | collective-permute-start | bytes 442376 | tf_op jit(solution)/shard_map/ppermute | solution.py:345
  70.6 17.4 %copy-start = (bf16[768,1536]{1,0:T(8,128)(2,1)S(1)}, bf16[768,1536]{1,0:T(8,128)(2,1)}, u32[]{:S(2)}) copy-start(bf16[768,1536]{1,0:T(8,128)(2,1)} %w_ref.7) | copy-start | bytes 7077892
  70.6 17.4 %copy-start.1 = (bf16[512,768]{1,0:T(8,128)(2,1)S(1)}, bf16[512,768]{1,0:T(8,128)(2,1)}, u32[]{:S(2)}) copy-start(bf16[512,768]{1,0:T(8,128)(2,1)} %get-tuple-element.60.attn_ref) | copy-start | bytes 2359300
  70.6 17.4 %copy-start.2 = (s32[12]{0:T(128)S(1)}, s32[12]{0:T(128)}, u32[]{:S(2)}) copy-start(s32[12]{0:T(128)} %concatenate.3.place_ref) | copy-start | bytes 148
  75.7 6.8 %collective-permute-start.14 = (bf16[48,1536]{1,0:T(8,128)(2,1)S(1)}, bf16[48,1536]{1,0:T(8,128)(2,1)S(1)}, u32[]{:S(2)}, u32[]{:S(2)}) collective-permute-start(bf16[48,1536]{1,0:T(8,128)(2,1)S(1)} %add_convert_fusion.2), channel_id=1, source_target_pairs={{0,128},{1,129},{2,130},{3,131},{4,132},{5,133},{6,134},{7,135},{8... | collective-permute-start | bytes 442376 | tf_op jit(solution)/shard_map/ppermute | solution.py:345
  77.9 6.1 %collective-permute-start.13 = (bf16[48,1536]{1,0:T(8,128)(2,1)S(1)}, bf16[48,1536]{1,0:T(8,128)(2,1)S(1)}, u32[]{:S(2)}, u32[]{:S(2)}) collective-permute-start(bf16[48,1536]{1,0:T(8,128)(2,1)S(1)} %add_convert_fusion.2), channel_id=1, source_target_pairs={{0,129},{1,128},{2,131},{3,130},{4,133},{5,132},{6,135},{7,134},{8... | collective-permute-start | bytes 442376 | tf_op jit(solution)/shard_map/ppermute | solution.py:345
  77.9 6.1 %collective-permute-start.12 = (bf16[48,1536]{1,0:T(8,128)(2,1)S(1)}, bf16[48,1536]{1,0:T(8,128)(2,1)S(1)}, u32[]{:S(2)}, u32[]{:S(2)}) collective-permute-start(bf16[48,1536]{1,0:T(8,128)(2,1)S(1)} %add_convert_fusion.2), channel_id=1, source_target_pairs={{0,1},{1,0},{2,3},{3,2},{4,5},{5,4},{6,7},{7,6},{8,9},{9,8},{10,11... | collective-permute-start | bytes 442376 | tf_op jit(solution)/shard_map/ppermute | solution.py:345
  80.4 7.5 %collective-permute-start.15 = (bf16[512,768]{1,0:T(8,128)(2,1)}, bf16[512,768]{1,0:T(8,128)(2,1)S(1)}, u32[]{:S(2)}, u32[]{:S(2)}) collective-permute-start(bf16[512,768]{1,0:T(8,128)(2,1)} %shard_map.97), channel_id=1, source_target_pairs={{0,64},{64,0},{1,65},{65,1},{2,66},{66,2},{3,67},{67,3},{4,68},{68... | collective-permute-start | bytes 2359304 | tf_op jit(solution)/shard_map/ppermute | solution.py:235
  84.1 9.3 %collective-permute-start.16 = (bf16[48,1536]{1,0:T(8,128)(2,1)S(1)}, bf16[48,1536]{1,0:T(8,128)(2,1)S(1)}, u32[]{:S(2)}, u32[]{:S(2)}) collective-permute-start(bf16[48,1536]{1,0:T(8,128)(2,1)S(1)} %add_convert_fusion.1), channel_id=1, source_target_pairs={{0,32},{1,33},{2,34},{3,35},{4,36},{5,37},{6,38},{7,39},{8,40},{9,... | collective-permute-start | bytes 442376 | tf_op jit(solution)/shard_map/ppermute | solution.py:345
  93.5 8.0 %collective-permute-start.20 = (bf16[48,1536]{1,0:T(8,128)(2,1)S(1)}, bf16[48,1536]{1,0:T(8,128)(2,1)S(1)}, u32[]{:S(2)}, u32[]{:S(2)}) collective-permute-start(bf16[48,1536]{1,0:T(8,128)(2,1)S(1)} %add_convert_fusion), channel_id=1, source_target_pairs={{0,16},{1,17},{2,18},{3,19},{4,20},{5,21},{6,22},{7,23},{8,56},{9,... | collective-permute-start | bytes 442376 | tf_op jit(solution)/shard_map/ppermute | solution.py:345
  96.5 8.6 %collective-permute-start.19 = (bf16[48,1536]{1,0:T(8,128)(2,1)S(1)}, bf16[48,1536]{1,0:T(8,128)(2,1)S(1)}, u32[]{:S(2)}, u32[]{:S(2)}) collective-permute-start(bf16[48,1536]{1,0:T(8,128)(2,1)S(1)} %add_convert_fusion), channel_id=1, source_target_pairs={{0,8},{1,9},{2,10},{3,11},{4,12},{5,13},{6,14},{7,15},{8,0},{9,1},... | collective-permute-start | bytes 442376 | tf_op jit(solution)/shard_map/ppermute | solution.py:345
  98.2 7.9 %collective-permute-start.18 = (bf16[48,1536]{1,0:T(8,128)(2,1)S(1)}, bf16[48,1536]{1,0:T(8,128)(2,1)S(1)}, u32[]{:S(2)}, u32[]{:S(2)}) collective-permute-start(bf16[48,1536]{1,0:T(8,128)(2,1)S(1)} %add_convert_fusion), channel_id=1, source_target_pairs={{0,56},{1,57},{2,58},{3,59},{4,60},{5,61},{6,62},{7,63},{8,16},{9,... | collective-permute-start | bytes 442376 | tf_op jit(solution)/shard_map/ppermute | solution.py:345
  98.3 23.3 %collective-permute-start.17 = (bf16[512,768]{1,0:T(8,128)(2,1)S(1)}, bf16[512,768]{1,0:T(8,128)(2,1)S(1)}, u32[]{:S(2)}, u32[]{:S(2)}) collective-permute-start(bf16[512,768]{1,0:T(8,128)(2,1)S(1)} %get-tuple-element.67), channel_id=1, source_target_pairs={{0,128},{128,0},{1,129},{129,1},{2,130},{130,2},{3,131},{131,3},{4... | collective-permute-start | bytes 2359304 | tf_op jit(solution)/shard_map/ppermute | solution.py:235
  106.2 10.0 %collective-permute-start.23 = (bf16[4,48,1536]{2,1,0:T(8,128)(2,1)S(1)}, bf16[4,48,1536]{2,1,0:T(8,128)(2,1)S(1)}, u32[]{:S(2)}, u32[]{:S(2)}) collective-permute-start(bf16[4,48,1536]{2,1,0:T(8,128)(2,1)S(1)} %pad_maximum_fusion.refs_0_), channel_id=1, source_target_pairs={{0,2},{1,3},{2,0},{3,1},{4,6},{5,7},{6,4},{7,5},{8,10},{9,11},{10,... | collective-permute-start | bytes 1769480 | tf_op jit(solution)/shard_map/ppermute | solution.py:345
  106.3 11.2 %collective-permute-start.21 = (bf16[4,48,1536]{2,1,0:T(8,128)(2,1)S(1)}, bf16[4,48,1536]{2,1,0:T(8,128)(2,1)S(1)}, u32[]{:S(2)}, u32[]{:S(2)}) collective-permute-start(bf16[4,48,1536]{2,1,0:T(8,128)(2,1)S(1)} %pad_maximum_fusion.refs_0_), channel_id=1, source_target_pairs={{0,6},{1,7},{2,4},{3,5},{4,2},{5,3},{6,0},{7,1},{8,14},{9,15},{10,... | collective-permute-start | bytes 1769480 | tf_op jit(solution)/shard_map/ppermute | solution.py:345
  116.2 8.0 %collective-permute-start.24 = (bf16[2,48,1536]{2,1,0:T(8,128)(2,1)S(1)}, bf16[2,48,1536]{2,1,0:T(8,128)(2,1)S(1)}, u32[]{:S(2)}, u32[]{:S(2)}) collective-permute-start(bf16[2,48,1536]{2,1,0:T(8,128)(2,1)S(1)} %slice.20), channel_id=1, source_target_pairs={{0,6},{1,7},{2,4},{3,5},{4,2},{5,3},{6,0},{7,1},{8,14},{9,15},{10,... | collective-permute-start | bytes 884744 | tf_op jit(solution)/shard_map/ppermute | solution.py:345
  117.5 6.8 %collective-permute-start.22 = (bf16[2,48,1536]{2,1,0:T(8,128)(2,1)S(1)}, bf16[2,48,1536]{2,1,0:T(8,128)(2,1)S(1)}, u32[]{:S(2)}, u32[]{:S(2)}) collective-permute-start(bf16[2,48,1536]{2,1,0:T(8,128)(2,1)S(1)} %slice.18), channel_id=1, source_target_pairs={{0,2},{1,3},{2,0},{3,1},{4,6},{5,7},{6,4},{7,5},{8,10},{9,11},{10,... | collective-permute-start | bytes 884744 | tf_op jit(solution)/shard_map/ppermute | solution.py:345
